TPU v7x, 32 devices: a whole 2x2x4 slice. The times are simulated.
32 devices in a mesh: rep: 2 (over core), shard: 16 (over z, y, x).
Axes of the slice: x: 2, y: 2, z: 4, core: 2. Of those that a mesh axis runs over, the one named last changes fastest.
Arguments:
- tokens: bfloat16 [4096, 640], P(('rep', 'shard')), may hold values from -6 to 6
- lengths: int32 [32, 2], P(('rep', 'shard')), may hold values from 0 to 128, as said below
- w_query: bfloat16 [640, 1024], P('shard'), may hold values from -0.25 to 0.25
- w_key: bfloat16 [640, 256], P('shard'), may hold values from -0.25 to 0.25
- w_value: bfloat16 [640, 256], P('shard'), may hold values from -0.25 to 0.25
- w_out: bfloat16 [1024, 640], P('shard'), may hold values from -0.1875 to 0.1875
- w_gate: bfloat16 [640, 2048], P('shard'), may hold values from -0.25 to 0.25
- w_up: bfloat16 [640, 2048], P('shard'), may hold values from -0.25 to 0.25
- w_down: bfloat16 [2048, 640], P('shard'), may hold values from -0.125 to 0.125
- norm_gains: bfloat16 [4, 640], P(None, 'shard'), may hold values from 0.25 to 1.75
- head_gains: bfloat16 [2, 256], P(None, 'shard'), may hold values from 0.69921875 to 2
- cotangent: bfloat16 [4096, 640], P(('rep', 'shard')), may hold values from -6 to 6
Outputs:
- mixed: bfloat16 [4096, 640], P(('rep', 'shard'))
- tokens_grad: bfloat16 [4096, 640], P(('rep', 'shard'))
- w_query_grad: float32 [640, 1024], P('shard')
- w_key_grad: float32 [640, 256], P('shard')
- w_value_grad: float32 [640, 256], P('shard')
- w_out_grad: float32 [1024, 640], P('shard')
- w_gate_grad: float32 [640, 2048], P('shard')
- w_up_grad: float32 [640, 2048], P('shard')
- w_down_grad: float32 [2048, 640], P('shard')
- norm_gains_grad: float32 [4, 640], P(None, 'shard')
- head_gains_grad: float32 [2, 256], P(None, 'shard')
Inputs may be any that keep to these rules, and one draw needn't show every extreme that they name: `lengths`: each row: first length at least 1, the two together between 64 and 128; in every draw one row holds a single sequence of 128 tokens and a second length of 0.
All inputs are finite; a program needn't handle non-finite values.
Results may differ from a plain program's by a relative error of at most 0.017.
Values may be sent and summed in bfloat16 or wider, within the bound.
A program may use at most 128 MiB of HBM per device.

v0:
```python
from functools import partial
import math

import jax
import jax.numpy as jnp
from jax import lax
from jax.sharding import PartitionSpec as P

HQ = 4
HD = 256


EPSILON = 1e-06
THETA = 1000000.0
QUERY_SCALE = 0.0625


def rms_norm(values, gain_row):
    return (
        values * lax.rsqrt(jnp.mean(values * values, axis=-1, keepdims=True) + EPSILON) * gain_row
    )


def rotary(values, cos_part, sin_part):
    midway = values.shape[-1] // 2
    leading = values[..., :midway]
    second = values[..., midway:]
    return jnp.concatenate(
        [leading * cos_part - second * sin_part, second * cos_part + leading * sin_part], axis=-1
    )


def layout(lengths, row_index):
    first_len = lengths[..., 0:1]
    second_len = lengths[..., 1:2]
    segment = (row_index >= first_len).astype(jnp.int32) + (
        row_index >= first_len + second_len
    ).astype(jnp.int32)
    offset = jnp.where(segment == 0, 0, jnp.where(segment == 1, first_len, first_len + second_len))
    return (segment, row_index - offset)


def angles(position, head_width):
    midway = head_width // 2
    frequency = jnp.exp(
        -(2.0 * jnp.arange(midway, dtype=jnp.float32) / head_width) * math.log(THETA)
    )
    phase_angle = position.astype(jnp.float32)[..., None] * frequency
    return (jnp.cos(phase_angle), jnp.sin(phase_angle))


def lead_dot(left, right):
    return lax.dot_general(
        left, right, (((0,), (0,)), ((), ())), preferred_element_type=jnp.float32
    )


def tail_dot(left, right):
    return lax.dot_general(
        left, right, (((1,), (1,)), ((), ())), preferred_element_type=jnp.float32
    )


def prepare_heads(cos_part, sin_part, query_raw, key_raw, query_gain, key_gain):
    query_heads = query_raw.reshape(query_raw.shape[0], HQ, HD)
    query_rot = (
        rotary(rms_norm(query_heads, query_gain), cos_part[:, None, :], sin_part[:, None, :])
        * QUERY_SCALE
    )
    key_rot = rotary(rms_norm(key_raw, key_gain), cos_part, sin_part)
    return (query_rot, key_rot)


def middle(token_f32, attn_proj, post_gain, pre_gain):
    resid = token_f32 + rms_norm(attn_proj, post_gain)
    return (resid, rms_norm(resid, pre_gain))


def geglu(gate_pre, up_pre):
    return jax.nn.gelu(gate_pre, approximate=True) * up_pre


def finish(live_mask, resid, down_out, final_gain):
    return (resid + rms_norm(down_out, final_gain)) * live_mask[:, None]


def block_scores(key_low, segment, row_index, query_block, seg_query, row_query):
    scores = jnp.einsum("qhd,kd->hqk", query_block, key_low, preferred_element_type=jnp.float32)
    allowed = (seg_query[:, None] == segment[None, :]) & (row_index[None, :] <= row_query[:, None])
    return jnp.where(allowed[None], scores, -1e30)


def attend_block(key_low, value_low, segment, row_index, inputs):
    query_block, seg_query, row_query = inputs
    scores = block_scores(key_low, segment, row_index, query_block, seg_query, row_query)
    top_score = jnp.max(scores, axis=-1, keepdims=True)
    expo = jnp.exp(scores - top_score)
    total = jnp.sum(expo, axis=-1, keepdims=True)
    probs = expo / total
    output = jnp.einsum(
        "hqk,kd->qhd", probs.astype(jnp.bfloat16), value_low, preferred_element_type=jnp.float32
    )
    return (output, top_score + jnp.log(total))


def attend_back(key_low, value_low, segment, row_index, running, inputs):
    key_grad, value_grad = running
    query_block, heads_block, seg_query, row_query, log_total = inputs
    scores = block_scores(key_low, segment, row_index, query_block, seg_query, row_query)
    probs = jnp.exp(scores - log_total)
    value_grad = value_grad + jnp.einsum(
        "hqk,qhd->kd", probs.astype(jnp.bfloat16), heads_block, preferred_element_type=jnp.float32
    )
    prob_grad = jnp.einsum(
        "qhd,kd->hqk", heads_block, value_low, preferred_element_type=jnp.float32
    )
    score_grad = (probs * (prob_grad - jnp.sum(probs * prob_grad, axis=-1, keepdims=True))).astype(
        jnp.bfloat16
    )
    query_grad = jnp.einsum("hqk,kd->qhd", score_grad, key_low, preferred_element_type=jnp.float32)
    key_grad = key_grad + jnp.einsum(
        "hqk,qhd->kd", score_grad, query_block, preferred_element_type=jnp.float32
    )
    return ((key_grad, value_grad), query_grad)


def local(
    tokens,
    lengths,
    w_query,
    w_key,
    w_value,
    w_out,
    w_gate,
    w_up,
    w_down,
    norm_gains,
    head_gains,
    cotangent,
):
    local_rows = tokens.shape[0]
    row_index = jnp.arange(local_rows, dtype=jnp.int32)
    segment, position = layout(lengths[0], row_index)
    live_mask = (segment < 2).astype(jnp.float32)
    cos_part, sin_part = angles(position, HD)
    gathered = (
        lax.all_gather(w_query, "shard", axis=0, tiled=True),
        lax.all_gather(w_key, "shard", axis=0, tiled=True),
        lax.all_gather(w_value, "shard", axis=0, tiled=True),
        lax.all_gather(w_out, "shard", axis=0, tiled=True),
        lax.all_gather(w_gate, "shard", axis=0, tiled=True),
        lax.all_gather(w_up, "shard", axis=0, tiled=True),
        lax.all_gather(w_down, "shard", axis=0, tiled=True),
        lax.all_gather(norm_gains, "shard", axis=1, tiled=True),
        lax.all_gather(head_gains, "shard", axis=1, tiled=True),
    )
    (
        full_query,
        full_key,
        full_value,
        full_out,
        full_gate,
        full_up,
        full_down,
        full_norms,
        full_heads,
    ) = gathered
    gains = full_norms.astype(jnp.float32)
    head_scale = full_heads.astype(jnp.float32)
    token_f32 = tokens.astype(jnp.float32)
    normed_in, input_back = jax.vjp(rms_norm, token_f32, gains[0])
    input_low = normed_in.astype(jnp.bfloat16)
    query_raw = jnp.dot(input_low, full_query, preferred_element_type=jnp.float32)
    key_raw = jnp.dot(input_low, full_key, preferred_element_type=jnp.float32)
    value_low = jnp.dot(input_low, full_value, preferred_element_type=jnp.float32).astype(
        jnp.bfloat16
    )
    (query_rot, key_rot), heads_back = jax.vjp(
        partial(prepare_heads, cos_part, sin_part), query_raw, key_raw, head_scale[0], head_scale[1]
    )
    query_low = query_rot.astype(jnp.bfloat16)
    key_low = key_rot.astype(jnp.bfloat16)
    block_rows = min(local_rows, 512)
    count = local_rows // block_rows
    query_blocks = query_low.reshape(count, block_rows, HQ, HD)
    seg_blocks = segment.reshape(count, block_rows)
    row_blocks = row_index.reshape(count, block_rows)
    outputs, log_totals = lax.map(
        partial(attend_block, key_low, value_low, segment, row_index),
        (query_blocks, seg_blocks, row_blocks),
    )
    attn_low = outputs.reshape(local_rows, HQ * HD).astype(jnp.bfloat16)
    attn_proj = jnp.dot(attn_low, full_out, preferred_element_type=jnp.float32)
    (resid, normed_mid), mid_back = jax.vjp(middle, token_f32, attn_proj, gains[1], gains[2])
    mid_low = normed_mid.astype(jnp.bfloat16)
    gate_pre = jnp.dot(mid_low, full_gate, preferred_element_type=jnp.float32)
    up_pre = jnp.dot(mid_low, full_up, preferred_element_type=jnp.float32)
    activated, glu_back = jax.vjp(geglu, gate_pre, up_pre)
    act_low = activated.astype(jnp.bfloat16)
    down_out = jnp.dot(act_low, full_down, preferred_element_type=jnp.float32)
    final, tail_back = jax.vjp(partial(finish, live_mask), resid, down_out, gains[3])
    mixed = final.astype(jnp.bfloat16)
    again = (
        lax.all_gather(w_query, "shard", axis=0, tiled=True),
        lax.all_gather(w_key, "shard", axis=0, tiled=True),
        lax.all_gather(w_value, "shard", axis=0, tiled=True),
        lax.all_gather(w_out, "shard", axis=0, tiled=True),
        lax.all_gather(w_gate, "shard", axis=0, tiled=True),
        lax.all_gather(w_up, "shard", axis=0, tiled=True),
        lax.all_gather(w_down, "shard", axis=0, tiled=True),
    )
    back_query, back_key, back_value, back_out, back_gate, back_up, back_down = again
    resid_grad, down_grad, final_gain_grad = tail_back(cotangent.astype(jnp.float32))
    down_low = down_grad.astype(jnp.bfloat16)
    grad_down = lead_dot(act_low, down_low)
    act_grad = tail_dot(down_low, back_down)
    gate_grad, up_grad = glu_back(act_grad)
    gate_low = gate_grad.astype(jnp.bfloat16)
    up_low = up_grad.astype(jnp.bfloat16)
    grad_gate = lead_dot(mid_low, gate_low)
    grad_up = lead_dot(mid_low, up_low)
    mid_grad = tail_dot(gate_low, back_gate) + tail_dot(up_low, back_up)
    token_grad_mid, attn_grad, post_gain_grad, pre_gain_grad = mid_back((resid_grad, mid_grad))
    attn_grad_low = attn_grad.astype(jnp.bfloat16)
    grad_out = lead_dot(attn_low, attn_grad_low)
    heads_grad = (
        tail_dot(attn_grad_low, back_out).astype(jnp.bfloat16).reshape(count, block_rows, HQ, HD)
    )
    zero_grad = jnp.zeros((local_rows, HD), jnp.float32)
    (key_grad, value_grad), query_grad = lax.scan(
        partial(attend_back, key_low, value_low, segment, row_index),
        (zero_grad, zero_grad),
        (query_blocks, heads_grad, seg_blocks, row_blocks, log_totals),
    )
    query_grad = query_grad.reshape(local_rows, HQ, HD)
    query_raw_grad, key_raw_grad, query_gain_grad, key_gain_grad = heads_back(
        (query_grad, key_grad)
    )
    query_low_grad = query_raw_grad.astype(jnp.bfloat16)
    key_low_grad = key_raw_grad.astype(jnp.bfloat16)
    value_low_grad = value_grad.astype(jnp.bfloat16)
    grad_query = lead_dot(input_low, query_low_grad)
    grad_key = lead_dot(input_low, key_low_grad)
    grad_value = lead_dot(input_low, value_low_grad)
    input_grad = (
        tail_dot(query_low_grad, back_query)
        + tail_dot(key_low_grad, back_key)
        + tail_dot(value_low_grad, back_value)
    )
    token_grad_in, in_gain_grad = input_back(input_grad)
    tokens_grad = (token_grad_mid + token_grad_in).astype(jnp.bfloat16)
    norm_grad = jnp.stack([in_gain_grad, post_gain_grad, pre_gain_grad, final_gain_grad])
    head_grad = jnp.stack([query_gain_grad, key_gain_grad])
    summed = (
        lax.psum_scatter(grad_query, "shard", scatter_dimension=0, tiled=True),
        lax.psum_scatter(grad_key, "shard", scatter_dimension=0, tiled=True),
        lax.psum_scatter(grad_value, "shard", scatter_dimension=0, tiled=True),
        lax.psum_scatter(grad_out, "shard", scatter_dimension=0, tiled=True),
        lax.psum_scatter(grad_gate, "shard", scatter_dimension=0, tiled=True),
        lax.psum_scatter(grad_up, "shard", scatter_dimension=0, tiled=True),
        lax.psum_scatter(grad_down, "shard", scatter_dimension=0, tiled=True),
        lax.psum_scatter(norm_grad, "shard", scatter_dimension=1, tiled=True),
        lax.psum_scatter(head_grad, "shard", scatter_dimension=1, tiled=True),
    )
    split = (
        lax.psum_scatter(
            summed[0].astype(jnp.bfloat16), "rep", scatter_dimension=1, tiled=True
        ).astype(jnp.float32),
        lax.psum_scatter(
            summed[1].astype(jnp.bfloat16), "rep", scatter_dimension=1, tiled=True
        ).astype(jnp.float32),
        lax.psum_scatter(
            summed[2].astype(jnp.bfloat16), "rep", scatter_dimension=1, tiled=True
        ).astype(jnp.float32),
        lax.psum_scatter(
            summed[3].astype(jnp.bfloat16), "rep", scatter_dimension=1, tiled=True
        ).astype(jnp.float32),
        lax.psum_scatter(
            summed[4].astype(jnp.bfloat16), "rep", scatter_dimension=1, tiled=True
        ).astype(jnp.float32),
        lax.psum_scatter(
            summed[5].astype(jnp.bfloat16), "rep", scatter_dimension=1, tiled=True
        ).astype(jnp.float32),
        lax.psum_scatter(
            summed[6].astype(jnp.bfloat16), "rep", scatter_dimension=1, tiled=True
        ).astype(jnp.float32),
    )
    gain_sums = lax.psum((summed[7], summed[8]), "rep")
    joined = (
        lax.all_gather(split[0].astype(jnp.bfloat16), "rep", axis=1, tiled=True).astype(
            jnp.float32
        ),
        lax.all_gather(split[1].astype(jnp.bfloat16), "rep", axis=1, tiled=True).astype(
            jnp.float32
        ),
        lax.all_gather(split[2].astype(jnp.bfloat16), "rep", axis=1, tiled=True).astype(
            jnp.float32
        ),
        lax.all_gather(split[3].astype(jnp.bfloat16), "rep", axis=1, tiled=True).astype(
            jnp.float32
        ),
        lax.all_gather(split[4].astype(jnp.bfloat16), "rep", axis=1, tiled=True).astype(
            jnp.float32
        ),
        lax.all_gather(split[5].astype(jnp.bfloat16), "rep", axis=1, tiled=True).astype(
            jnp.float32
        ),
        lax.all_gather(split[6].astype(jnp.bfloat16), "rep", axis=1, tiled=True).astype(
            jnp.float32
        ),
    )
    results = (
        joined[0],
        joined[1],
        joined[2],
        joined[3],
        joined[4],
        joined[5],
        joined[6],
        gain_sums[0],
        gain_sums[1],
    )
    return (
        mixed,
        tokens_grad,
        results[0],
        results[1],
        results[2],
        results[3],
        results[4],
        results[5],
        results[6],
        results[7],
        results[8],
    )


def solution(mesh):
    placed = (
        P(("rep", "shard"), None),
        P(("rep", "shard"), None),
        P("shard", None),
        P("shard", None),
        P("shard", None),
        P("shard", None),
        P("shard", None),
        P("shard", None),
        P("shard", None),
        P(None, "shard"),
        P(None, "shard"),
        P(("rep", "shard"), None),
    )
    return jax.shard_map(
        local,
        mesh=mesh,
        in_specs=placed,
        out_specs=(
            P(("rep", "shard"), None),
            P(("rep", "shard"), None),
            P("shard", None),
            P("shard", None),
            P("shard", None),
            P("shard", None),
            P("shard", None),
            P("shard", None),
            P("shard", None),
            P(None, "shard"),
            P(None, "shard"),
        ),
        check_vma=False,
    )
```

profile of v0, /device:TPU:9, one launch (start us, length us, event | category | flops | bytes accessed | tf_op | source)
XLA Modules:
  0.0 1173.3 jit_solution(6526135451749404648)
XLA Ops:
  13.0 27.3 %all-gather.1 = bf16[16,16,2]{1,2,0:T(2,128)(2,1)S(1)} all-gather(bf16[1,16,2]{1,2,0:T(2,128)(2,1)} %bitcast.156), channel_id=1, replica_groups=mesh['rep'=2,'shard'=16] {'shard'}, dimensions={0}, use_global_device_ids=true | all-gather | bytes 1088 | tf_op jit(solution)/shard_map/all_gather | solution.py:155
  40.3 30.0 %all-gather = bf16[16,40,4]{1,2,0:T(4,128)(2,1)S(1)} all-gather(bf16[1,40,4]{1,2,0:T(4,128)(2,1)} %bitcast.155), channel_id=1, replica_groups=mesh['rep'=2,'shard'=16] {'shard'}, dimensions={0}, use_global_device_ids=true | all-gather | bytes 5440 | tf_op jit(solution)/shard_map/all_gather | solution.py:154
  70.4 32.7 %all_gather.57 = bf16[640,256]{1,0:T(8,128)(2,1)S(1)} all-gather(bf16[40,256]{1,0:T(8,128)(2,1)} %param.15), channel_id=1, replica_groups=mesh['rep'=2,'shard'=16] {'shard'}, dimensions={0}, use_global_device_ids=true | all-gather | bytes 348160 | tf_op jit(solution)/shard_map/all_gather | solution.py:148
  103.2 1.4 multiply_reduce_fusion.14
  104.6 30.4 %all_gather.56 = bf16[640,256]{1,0:T(8,128)(2,1)S(1)} all-gather(bf16[40,256]{1,0:T(8,128)(2,1)} %param.16), channel_id=1, replica_groups=mesh['rep'=2,'shard'=16] {'shard'}, dimensions={0}, use_global_device_ids=true | all-gather | bytes 348160 | tf_op jit(solution)/shard_map/all_gather | solution.py:149
  140.1 1.8 fusion.79
  143.9 1.9 multiply_reduce_fusion.10
  146.7 48.3 %all-gather.13.cloned.1.call-done = bf16[640,2048]{1,0:T(8,128)(2,1)} async-done(((bf16[40,2048]{1,0:T(8,128)(2,1)}), bf16[640,2048]{1,0:T(8,128)(2,1)}) %all-gather.13.cloned.1.call-update) | async-done | bytes 2621456 | tf_op jit(solution)/shard_map/all_gather | solution.py:151
  195.0 2.3 fusion.87
  197.4 63.2 %all-gather.15.cloned.1.call-done = bf16[640,2048]{1,0:T(8,128)(2,1)} async-done(((bf16[40,2048]{1,0:T(8,128)(2,1)}), bf16[640,2048]{1,0:T(8,128)(2,1)}) %all-gather.15.cloned.1.call-update) | async-done | bytes 2621456 | tf_op jit(solution)/shard_map/all_gather | solution.py:152
  260.6 3.5 multiply_convert_fusion.1
  264.0 62.0 %all-gather.17.cloned.1.call-done = bf16[2048,640]{1,0:T(8,128)(2,1)} async-done(((bf16[128,640]{1,0:T(8,128)(2,1)}), bf16[2048,640]{1,0:T(8,128)(2,1)}) %all-gather.17.cloned.1.call-update) | async-done | bytes 2621456 | tf_op jit(solution)/shard_map/all_gather | solution.py:153
  326.1 2.6 multiply_reduce_fusion.8
  328.7 2.1 multiply_reduce_fusion.2
  330.8 1.4 multiply_convert_fusion
  334.4 1.6 multiply_reduce_fusion.3
  344.3 2.0 fusion.90
  347.7 2.1 fusion.77
  349.9 3.3 fusion.69
  354.2 3.2 fusion.92
  358.5 3.2 fusion.91
  362.7 36.4 %reduce-scatter.33.cloned.1.call-done = f32[40,256]{1,0:T(8,128)} async-done(((f32[640,256]{1,0:T(8,128)}), f32[40,256]{1,0:T(8,128)}) %reduce-scatter.33.cloned.1.call-update) | async-done | bytes 40976 | tf_op jit(solution)/shard_map/reduce_scatter | solution.py:257
  400.7 73.9 %reduce-scatter.31.cloned.1.call-done = f32[40,256]{1,0:T(8,128)} async-done(((f32[640,256]{1,0:T(8,128)}), f32[40,256]{1,0:T(8,128)}) %reduce-scatter.31.cloned.1.call-update) | async-done | bytes 40976 | tf_op jit(solution)/shard_map/reduce_scatter | solution.py:256
  477.5 78.9 %reduce-scatter.35.cloned.1.call-done = f32[64,640]{1,0:T(8,128)} async-done(((f32[1024,640]{1,0:T(8,128)}), f32[64,640]{1,0:T(8,128)}) %reduce-scatter.35.cloned.1.call-update) | async-done | bytes 163856 | tf_op jit(solution)/shard_map/reduce_scatter | solution.py:258
  558.8 78.8 %reduce-scatter.27.cloned.1.call-done = f32[40,1024]{1,0:T(8,128)} async-done(((f32[640,1024]{1,0:T(8,128)}), f32[40,1024]{1,0:T(8,128)}) %reduce-scatter.27.cloned.1.call-update) | async-done | bytes 163856 | tf_op jit(solution)/shard_map/reduce_scatter | solution.py:255
  637.6 1.5 convert_element_type.210
  639.5 128.4 %reduce-scatter.45.cloned.1.call-done = f32[128,640]{1,0:T(8,128)} async-done(((f32[2048,640]{1,0:T(8,128)}), f32[128,640]{1,0:T(8,128)}) %reduce-scatter.45.cloned.1.call-update) | async-done | bytes 327696 | tf_op jit(solution)/shard_map/reduce_scatter | solution.py:261
  770.1 61.0 %all-reduce.4 = f32[4,640]{1,0:T(4,128)S(1)} all-reduce(f32[4,640]{1,0:T(4,128)S(1)} %pad_maximum_fusion), channel_id=16, replica_groups=mesh['rep'=2,'shard'=16] {'shard'}, use_global_device_ids=true, to_apply=%region_33.34.clone | all-reduce | flops 2560 | bytes 20480
  831.1 58.0 %reduce-scatter.41.cloned.1.call-done = f32[40,2048]{1,0:T(8,128)} async-done(((f32[640,2048]{1,0:T(8,128)}), f32[40,2048]{1,0:T(8,128)}) %reduce-scatter.41.cloned.1.call-update) | async-done | bytes 327696 | tf_op jit(solution)/shard_map/reduce_scatter | solution.py:260
  889.2 1.7 convert_element_type.220
  891.0 116.6 %reduce-scatter.37.cloned.1.call-done = f32[40,2048]{1,0:T(8,128)} async-done(((f32[640,2048]{1,0:T(8,128)}), f32[40,2048]{1,0:T(8,128)}) %reduce-scatter.37.cloned.1.call-update) | async-done | bytes 327696 | tf_op jit(solution)/shard_map/reduce_scatter | solution.py:259
  1007.6 1.7 convert_element_type.218
  1010.1 61.1 %reduce-scatter.55.cloned.1.call-done = f32[16,2]{1,0:T(8,128)} async-done(((f32[256,2]{1,0:T(8,128)}), f32[16,2]{1,0:T(8,128)}) %reduce-scatter.55.cloned.1.call-update) | async-done | bytes 144
  1071.9 15.1 %all-reduce.5 = (f32[4,40]{1,0:T(4,128)}, f32[2,16]{1,0:T(2,128)}) all-reduce(f32[4,40]{1,0:T(4,128)S(1)} %constant_dynamic-slice_fusion, f32[2,16]{1,0:T(2,128)S(1)} %copy.120), channel_id=1, replica_groups=mesh['rep'=2,'shard'=16] {'rep'}, use_global_device_ids=true, to_apply=%region_34.35 | all-reduce | flops 192 | bytes 1536 | tf_op jit(solution)/shard_map/psum | solution.py:288
  1087.0 8.9 reduce-scatter.49.cloned.1.call-done
  1096.8 1.8 all_gather.66
  1099.2 7.5 reduce-scatter.47.cloned.1.call-done
  1107.5 1.8 all_gather.65
  1110.0 8.2 reduce-scatter.51.cloned.1.call-done
  1119.2 1.9 all-gather.2
  1122.0 7.0 reduce-scatter.29.cloned.1.call-done
  1128.9 2.3 all_gather.64
  1131.9 8.5 reduce-scatter.53.cloned.1.call-done
  1140.4 2.1 all_gather.70
  1143.4 8.6 reduce-scatter.43.cloned.1.call-done
  1152.0 2.3 all_gather.69
  1155.0 8.4 reduce-scatter.39.cloned.1.call-done
  1163.5 2.3 all_gather.68
  (277 shorter events, 45.1 us)
Async XLA Ops:
  7.2 132.9 %copy-start = (bf16[128,640]{1,0:T(8,128)(2,1)S(1)}, bf16[128,640]{1,0:T(8,128)(2,1)}, u32[]{:S(2)}) copy-start(bf16[128,640]{1,0:T(8,128)(2,1)} %param.12) | copy-start | bytes 491524
  7.2 132.9 %all-gather.9.cloned.1.call-start = ((), (), s32[]{:S(2)}) async-start(), calls=%async_computation.15 | async-start | bytes 1392640 | tf_op jit(solution)/shard_map/all_gather | solution.py:147
  7.9 135.9 %all-gather.11.cloned.1.call-start = ((), (), s32[]{:S(2)}) async-start(), calls=%async_computation.16 | async-start | bytes 1392640 | tf_op jit(solution)/shard_map/all_gather | solution.py:150
  8.7 186.4 %all-gather.13.cloned.1.call-start = ((), (), s32[]{:S(2)}) async-start(), calls=%async_computation.17 | async-start | bytes 2785280 | tf_op jit(solution)/shard_map/all_gather | solution.py:151
  9.4 251.1 %all-gather.15.cloned.1.call-start = ((), (), s32[]{:S(2)}) async-start(), calls=%async_computation.18 | async-start | bytes 2785280 | tf_op jit(solution)/shard_map/all_gather | solution.py:152
  10.0 316.1 %all-gather.17.cloned.1.call-start = ((), (), s32[]{:S(2)}) async-start(), calls=%async_computation.19 | async-start | bytes 2785280 | tf_op jit(solution)/shard_map/all_gather | solution.py:153
  10.6 388.5 %reduce-scatter.33.cloned.1.call-start = ((), (), s32[]{:S(2)}) async-start(), calls=%async_computation.23 | async-start | bytes 696320 | tf_op jit(solution)/shard_map/reduce_scatter | solution.py:257
  10.6 129.5 %copy-start.58 = (f32[128]{0:T(128)}, f32[128]{0:T(128)S(1)}, u32[]{:S(2)}) copy-start(f32[128]{0:T(128)S(1)} %multiply_exponential_fusion) | copy-start | bytes 1540
  11.7 28.6 %copy-start.62 = (f32[128]{0:T(128)}, f32[128]{0:T(128)S(1)}, u32[]{:S(2)}) copy-start(f32[128]{0:T(128)S(1)} %fusion.23) | copy-start | bytes 1540
  11.7 128.4 %copy-start.36 = (f32[128]{0:T(128)}, f32[128]{0:T(128)S(1)}, u32[]{:S(2)}) copy-start(f32[128]{0:T(128)S(1)} %fusion.58) | copy-start | bytes 1540
  103.2 36.8 %copy-start.13 = (bf16[640,256]{1,0:T(8,128)(2,1)}, bf16[640,256]{1,0:T(8,128)(2,1)S(1)}, u32[]{:S(2)}) copy-start(bf16[640,256]{1,0:T(8,128)(2,1)S(1)} %all_gather.57) | copy-start | bytes 983044
  104.5 32.4 %copy-start.71 = (f32[128]{0:T(128)}, f32[128]{0:T(128)S(1)}, u32[]{:S(2)}) copy-start(f32[128]{0:T(128)S(1)} %get-tuple-element.153) | copy-start | bytes 1540
  104.5 35.6 %copy-start.17 = (f32[128,256]{1,0:T(8,128)}, f32[128,256]{1,0:T(8,128)S(1)}, u32[]{:S(2)}) copy-start(f32[128,256]{1,0:T(8,128)S(1)} %get-tuple-element.154) | copy-start | bytes 393220
  104.6 35.4 %copy-start.50 = (f32[128]{0:T(128)}, f32[128]{0:T(128)S(1)}, u32[]{:S(2)}) copy-start(f32[128]{0:T(128)S(1)} %fusion.59) | copy-start | bytes 1540
  135.0 5.0 copy-start.15
  146.0 51.3 %copy-start.54 = (f32[128]{0:T(128)}, f32[128]{0:T(128)S(1)}, u32[]{:S(2)}) copy-start(f32[128]{0:T(128)S(1)} %fusion.61) | copy-start | bytes 1540
  264.0 64.6 %copy-start.12 = (bf16[128,640]{1,0:T(8,128)(2,1)S(1)}, bf16[128,640]{1,0:T(8,128)(2,1)}, u32[]{:S(2)}) copy-start(bf16[128,640]{1,0:T(8,128)(2,1)} %param.23) | copy-start | bytes 491524
  326.1 4.7 copy-start.24
  326.1 4.7 copy-start.48
  337.6 4.7 copy-start.57
  337.7 5.0 copy-start.18
  337.7 5.0 copy-start.42
  337.7 5.0 copy-start.51
  337.7 5.2 copy-start.72
  337.7 5.3 copy-start.38
  338.9 5.4 copy-start.20
  340.1 134.5 %reduce-scatter.31.cloned.1.call-start = ((), (), s32[]{:S(2)}) async-start(), calls=%async_computation.22 | async-start | bytes 696320 | tf_op jit(solution)/shard_map/reduce_scatter | solution.py:256
  344.3 212.2 %reduce-scatter.35.cloned.1.call-start = ((), (), s32[]{:S(2)}) async-start(), calls=%async_computation.24 | async-start | bytes 2785280 | tf_op jit(solution)/shard_map/reduce_scatter | solution.py:258
  346.4 291.2 %reduce-scatter.27.cloned.1.call-start = ((), (), s32[]{:S(2)}) async-start(), calls=%async_computation.20 | async-start | bytes 2785280 | tf_op jit(solution)/shard_map/reduce_scatter | solution.py:255
  349.8 418.0 %reduce-scatter.45.cloned.1.call-start = ((), (), s32[]{:S(2)}) async-start(), calls=%async_computation.29 | async-start | bytes 5570560 | tf_op jit(solution)/shard_map/reduce_scatter | solution.py:261
  353.2 535.9 %reduce-scatter.41.cloned.1.call-start = ((), (), s32[]{:S(2)}) async-start(), calls=%async_computation.27 | async-start | bytes 5570560 | tf_op jit(solution)/shard_map/reduce_scatter | solution.py:260
  357.5 650.1 %reduce-scatter.37.cloned.1.call-start = ((), (), s32[]{:S(2)}) async-start(), calls=%async_computation.25 | async-start | bytes 5570560 | tf_op jit(solution)/shard_map/reduce_scatter | solution.py:259
  361.7 114.5 %copy-start.70 = (u32[32]{0:T(128)S(1)}, u32[32]{0:T(128)}, u32[]{:S(2)}) copy-start(u32[32]{0:T(128)} %constant.109) | copy-start | bytes 388
  361.7 115.7 %copy-start.43 = (f32[640]{0:T(1024)S(1)}, f32[640]{0:T(1024)}, u32[]{:S(2)}) copy-start(f32[640]{0:T(1024)} %get-tuple-element.119) | copy-start | bytes 7684
  361.7 115.7 %copy-start.44 = (f32[640]{0:T(1024)S(1)}, f32[640]{0:T(1024)}, u32[]{:S(2)}) copy-start(f32[640]{0:T(1024)} %get-tuple-element.117) | copy-start | bytes 7684
  361.7 115.8 %copy-start.45 = (f32[640]{0:T(1024)S(1)}, f32[640]{0:T(1024)}, u32[]{:S(2)}) copy-start(f32[640]{0:T(1024)} %get-tuple-element.115) | copy-start | bytes 7684
  361.7 196.5 %copy-start.3 = (bf16[640,1024]{1,0:T(8,128)(2,1)S(1)}, bf16[640,1024]{1,0:T(8,128)(2,1)}, u32[]{:S(2)}) copy-start(bf16[640,1024]{1,0:T(8,128)(2,1)} %all-gather.9.cloned.1.call-done) | copy-start | bytes 3932164
  361.8 277.4 %copy-start.14 = (bf16[640,256]{1,0:T(8,128)(2,1)S(1)}, bf16[640,256]{1,0:T(8,128)(2,1)}, u32[]{:S(2)}) copy-start(bf16[640,256]{1,0:T(8,128)(2,1)} %copy-done.13) | copy-start | bytes 983044
  361.8 709.4 %reduce-scatter.55.cloned.1.call-start = ((), (), s32[]{:S(2)}) async-start(), calls=%async_computation.34 | async-start | bytes 139264
  362.7 733.3 %reduce-scatter.49.cloned.1.call-start = ((), (), s32[]{:S(2)}) async-start(), calls=%async_computation.31 | async-start | bytes 98304
  400.6 369.1 %copy-start.16 = (bf16[640,256]{1,0:T(8,128)(2,1)S(1)}, bf16[640,256]{1,0:T(8,128)(2,1)}, u32[]{:S(2)}) copy-start(bf16[640,256]{1,0:T(8,128)(2,1)} %copy-done.15) | copy-start | bytes 983044
  400.6 706.0 %reduce-scatter.47.cloned.1.call-start = ((), (), s32[]{:S(2)}) async-start(), calls=%async_computation.30 | async-start | bytes 98304
  476.1 642.0 %reduce-scatter.51.cloned.1.call-start = ((), (), s32[]{:S(2)}) async-start(), calls=%async_computation.32 | async-start | bytes 245760
  558.2 570.7 %reduce-scatter.29.cloned.1.call-start = ((), (), s32[]{:S(2)}) async-start(), calls=%async_computation.21 | async-start | bytes 122880 | tf_op jit(solution)/shard_map/reduce_scatter | solution.py:266
  558.8 332.1 %copy-start.63 = (f32[128]{0:T(128)S(1)}, f32[128]{0:T(128)}, u32[]{:S(2)}) copy-start(f32[128]{0:T(128)} %copy-done.62) | copy-start | bytes 1540
  639.2 501.2 %reduce-scatter.53.cloned.1.call-start = ((), (), s32[]{:S(2)}) async-start(), calls=%async_computation.33 | async-start | bytes 245760
  769.7 382.3 %reduce-scatter.43.cloned.1.call-start = ((), (), s32[]{:S(2)}) async-start(), calls=%async_computation.28 | async-start | bytes 245760 | tf_op jit(solution)/shard_map/reduce_scatter | solution.py:281
  890.8 272.6 %reduce-scatter.39.cloned.1.call-start = ((), (), s32[]{:S(2)}) async-start(), calls=%async_computation.26 | async-start | bytes 245760 | tf_op jit(solution)/shard_map/reduce_scatter | solution.py:278
  (45 other events, 104.5 us)
Sparse Core Ops, SparseCore 0:
  10.8 55.9 all-gather.8
  69.5 57.1 all-gather.10
  129.4 65.5 all-gather.12
  197.6 62.9 all-gather.14
  263.1 62.9 all-gather.16
  340.2 58.8 reduce-scatter.32
  401.4 73.1 reduce-scatter.30
  476.9 79.5 reduce-scatter.34
  558.7 78.7 reduce-scatter.26
  639.7 128.0 reduce-scatter.44
  770.2 118.9 reduce-scatter.40
  891.3 116.2 reduce-scatter.36
  1010.4 60.7 reduce-scatter.54
  1073.3 22.6 reduce-scatter.48
  1098.0 8.5 reduce-scatter.46
  1109.4 8.7 reduce-scatter.50
  1120.3 8.6 reduce-scatter.28
  1131.7 8.6 reduce-scatter.52
  1143.3 8.7 reduce-scatter.42
  1154.7 8.6 reduce-scatter.38
where the time goes:
time: 1180 us; the launch traced here: 1170 us
  waiting for transfers between devices  866 us (73%)
  blocking collectives  211 us (18%)
  matrix products  39.4 us (3%)
  other arithmetic  22.6 us (2%)
  between operations  17.5 us (1%)
  local copies, waits for them, and re-layouts  15.8 us (1%)
    reduce_scatter x1, waiting for transfers between devices, local(): lax.psum_scatter(grad_down, 'shard', scatter_dimension=0, tiled=True)  128 us
    reduce_scatter x1, waiting for transfers between devices, local(): lax.psum_scatter(grad_gate, 'shard', scatter_dimension=0, tiled=True)  117 us
    unnamed x25, waiting for transfers between devices  97.6 us
    reduce_scatter x1, waiting for transfers between devices, local(): lax.psum_scatter(grad_out, 'shard', scatter_dimension=0, tiled=True)  78.9 us
    reduce_scatter x1, waiting for transfers between devices, local(): lax.psum_scatter(grad_query, 'shard', scatter_dimension=0, tiled=True)  78.8 us
    reduce_scatter x1, waiting for transfers between devices, local(): lax.psum_scatter(grad_key, 'shard', scatter_dimension=0, tiled=True)  73.9 us
    all_gather x1, waiting for transfers between devices, local(): lax.all_gather(w_up, 'shard', axis=0, tiled=True)  63.2 us
    all_gather x1, waiting for transfers between devices, local(): lax.all_gather(w_down, 'shard', axis=0, tiled=True)  62 us
  transfers between devices with their start and end apart: 20, of which 18 were waited for; matrix products, arithmetic and copies ran while one was open for 5% of the time, Pallas kernels for 0%

commit v1 on v0

v1 whole, which is shorter than its diff:
```python
from functools import partial
import math

import jax
import jax.numpy as jnp
from jax import lax
from jax.experimental import pallas as pl
from jax.experimental.pallas import tpu as pltpu
from jax.sharding import PartitionSpec as P

HQ = 4
HD = 256


EPSILON = 1e-06
THETA = 1000000.0
QUERY_SCALE = 0.0625


def rms_norm(values, gain_row):
    return (
        values * lax.rsqrt(jnp.mean(values * values, axis=-1, keepdims=True) + EPSILON) * gain_row
    )


def rotary(values, cos_part, sin_part):
    midway = values.shape[-1] // 2
    leading = values[..., :midway]
    second = values[..., midway:]
    return jnp.concatenate(
        [leading * cos_part - second * sin_part, second * cos_part + leading * sin_part], axis=-1
    )


def layout(lengths, row_index):
    first_len = lengths[..., 0:1]
    second_len = lengths[..., 1:2]
    segment = (row_index >= first_len).astype(jnp.int32) + (
        row_index >= first_len + second_len
    ).astype(jnp.int32)
    offset = jnp.where(segment == 0, 0, jnp.where(segment == 1, first_len, first_len + second_len))
    return (segment, row_index - offset)


def angles(position, head_width):
    midway = head_width // 2
    frequency = jnp.exp(
        -(2.0 * jnp.arange(midway, dtype=jnp.float32) / head_width) * math.log(THETA)
    )
    phase_angle = position.astype(jnp.float32)[..., None] * frequency
    return (jnp.cos(phase_angle), jnp.sin(phase_angle))


def lead_dot(left, right):
    return lax.dot_general(
        left, right, (((0,), (0,)), ((), ())), preferred_element_type=jnp.float32
    )


def tail_dot(left, right):
    return lax.dot_general(
        left, right, (((1,), (1,)), ((), ())), preferred_element_type=jnp.float32
    )


def prepare_heads(cos_part, sin_part, query_raw, key_raw, query_gain, key_gain):
    query_heads = query_raw.reshape(query_raw.shape[0], HQ, HD)
    query_rot = (
        rotary(rms_norm(query_heads, query_gain), cos_part[:, None, :], sin_part[:, None, :])
        * QUERY_SCALE
    )
    key_rot = rotary(rms_norm(key_raw, key_gain), cos_part, sin_part)
    return (query_rot, key_rot)


def middle(token_f32, attn_proj, post_gain, pre_gain):
    resid = token_f32 + rms_norm(attn_proj, post_gain)
    return (resid, rms_norm(resid, pre_gain))


def geglu(gate_pre, up_pre):
    return jax.nn.gelu(gate_pre, approximate=True) * up_pre


def finish(live_mask, resid, down_out, final_gain):
    return (resid + rms_norm(down_out, final_gain)) * live_mask[:, None]


def causal_mask(segment, row_index):
    return (segment[:, None] == segment[None, :]) & (row_index[None, :] <= row_index[:, None])


MESH = pl.DeviceIdType.MESH


def place():
    core = lax.axis_index("rep")
    me = lax.axis_index("shard")
    x = lax.rem(me, 2)
    y = lax.rem(me // 2, 2)
    z = me // 4

    def index(dz, first, second):
        flip_y = (1 - core) * first + core * second
        flip_x = core * first + (1 - core) * second
        ny = y + flip_y * (1 - 2 * y)
        nx = x + flip_x * (1 - 2 * x)
        return (lax.rem(z + dz, 4) * 2 + ny) * 2 + nx

    return core, me, index


def greet(core, me, index):
    barrier = pltpu.get_barrier_semaphore()
    partners = [(core, index(dz, 0, 0)) for dz in (1, 2, 3)]
    partners += [(core, index(0, 1, 0)), (core, index(0, 0, 1)), (1 - core, me)]
    for partner in partners:
        pl.semaphore_signal(barrier, inc=1, device_id=partner, device_id_type=MESH)
    pl.semaphore_wait(barrier, len(partners))


def gather_kernel(wide_in, tall_in, wide_out, tall_out, local_sem, send_sem, recv_sem):
    core, me, index = place()
    greet(core, me, index)
    pairs = ((wide_in, wide_out), (tall_in, tall_out))
    sent = []
    slot = [0]

    def send(block, target, own=False):
        for n, (source, dest) in enumerate(pairs):
            copy = pltpu.make_async_remote_copy(
                src_ref=source.at[core] if own else dest.at[core, block],
                dst_ref=dest.at[core, block],
                send_sem=send_sem.at[n, slot[0]],
                recv_sem=recv_sem.at[n, core, block],
                device_id=target,
                device_id_type=MESH,
            )
            copy.start()
            sent.append(copy)
        slot[0] += 1

    def arrive(half, block):
        for n, (_, dest) in enumerate(pairs):
            pltpu.make_async_remote_copy(
                src_ref=dest.at[half, block],
                dst_ref=dest.at[half, block],
                send_sem=send_sem.at[n, 0],
                recv_sem=recv_sem.at[n, half, block],
                device_id=(1 - core, me),
                device_id_type=MESH,
            ).wait_recv()

    first, second, other = (core, index(0, 1, 0)), (core, index(0, 0, 1)), (1 - core, me)
    for dz in (2, 1, 3):
        send(me, (core, index(dz, 0, 0)), True)
    send(me, second, True)
    send(me, first, True)
    kept = []
    for n, (source, dest) in enumerate(pairs):
        for half in (0, 1):
            copy = pltpu.make_async_copy(source.at[half], dest.at[half, me], local_sem.at[n, half])
            copy.start()
            kept.append(copy)
    ranks = (1, 3, 2)
    for dz in ranks:
        block = index(dz, 0, 0)
        arrive(core, block)
        send(block, second)
        send(block, first)
        send(block, other)
    for dz in (0,) + ranks:
        block = index(dz, 1, 0)
        arrive(core, block)
        send(block, second)
        send(block, other)
    for flip in (0, 1):
        for dz in (0,) + ranks:
            block = index(dz, flip, 1)
            arrive(core, block)
            send(block, other)
    for step in range(1, 16):
        arrive(1 - core, lax.rem(me + step, 16))
    for copy in kept:
        copy.wait()
    for copy in sent:
        copy.wait_send()


def gather_parts(wide, tall):
    return pl.pallas_call(
        gather_kernel,
        out_shape=(
            jax.ShapeDtypeStruct((2, 16) + wide.shape[1:], wide.dtype),
            jax.ShapeDtypeStruct((2, 16) + tall.shape[1:], tall.dtype),
        ),
        in_specs=[pl.BlockSpec(memory_space=pl.ANY)] * 2,
        out_specs=(pl.BlockSpec(memory_space=pl.ANY),) * 2,
        scratch_shapes=[
            pltpu.SemaphoreType.DMA((2, 2)),
            pltpu.SemaphoreType.DMA((2, 30)),
            pltpu.SemaphoreType.DMA((2, 2, 16)),
        ],
        compiler_params=pltpu.CompilerParams(collective_id=0, has_side_effects=True),
        name="gather_weights",
    )(wide, tall)


def scatter_kernel(wide_in, tall_in, wide_out, tall_out, *scratch):
    core, me, index = place()
    wide_buffers, tall_buffers = scratch[0:5], scratch[5:10]
    send_sem, recv_sem = scratch[10:12]
    greet(core, me, index)
    arrays = (
        (wide_in, wide_out) + tuple(wide_buffers),
        (tall_in, tall_out) + tuple(tall_buffers),
    )
    sent = []
    slot = [0]
    other = (1 - core, me)

    def send(pick_source, pick_dest, receive, target):
        for n, refs in enumerate(arrays):
            copy = pltpu.make_async_remote_copy(
                src_ref=pick_source(refs),
                dst_ref=pick_dest(refs),
                send_sem=send_sem.at[n, slot[0]],
                recv_sem=recv_sem.at[n, receive],
                device_id=target,
                device_id_type=MESH,
            )
            copy.start()
            sent.append(copy)
        slot[0] += 1

    def arrive(pick, receive):
        for n, refs in enumerate(arrays):
            pltpu.make_async_remote_copy(
                src_ref=pick(refs),
                dst_ref=pick(refs),
                send_sem=send_sem.at[n, 0],
                recv_sem=recv_sem.at[n, receive],
                device_id=other,
                device_id_type=MESH,
            ).wait_recv()

    order = (2, 1, 3, 0)
    position = 0
    for turned, straight in ((1, 0), (1, 1), (0, 1), (0, 0)):
        for dz in order:
            block = index(dz, turned, straight)
            send(
                lambda refs, block=block: refs[0].at[1 - core, block],
                lambda refs, at=position: refs[2].at[at],
                position,
                other,
            )
            position += 1

    position = 0
    for group, (turned, straight) in enumerate(((0, 1), (1, 1), (1, 0), (0, 0))):
        for rank, dz in enumerate(order):
            block = index(dz, turned, straight)
            incoming = [(2, position)]
            if group >= 2:
                incoming.append((3, {2: 4, 3: 0}[group] + rank))
            if group == 3:
                incoming.append((4, rank))
            bases = {2: 0, 3: 16, 4: 24, 5: 28}
            last = group == 3 and dz == 0
            if last:
                incoming += [(5, 0), (5, 1), (5, 2)]
            for which, at in incoming:
                arrive(lambda refs, which=which, at=at: refs[which].at[at], bases[which] + at)
            for refs in arrays:
                total = refs[0][core, block].astype(jnp.float32)
                for which, at in incoming:
                    total = total + refs[which][at].astype(jnp.float32)
                if last:
                    refs[1][core] = total.astype(jnp.bfloat16)
                else:
                    refs[6][position] = total.astype(jnp.bfloat16)
            source = lambda refs, at=position: refs[6].at[at]
            if group < 2:
                at = group * 4 + rank
                send(source, lambda refs, at=at: refs[3].at[at], 16 + at, (core, index(0, 0, 1)))
            elif group == 2:
                send(source, lambda refs, at=rank: refs[4].at[at], 24 + rank, (core, index(0, 1, 0)))
            elif not last:
                send(source, lambda refs, at=rank: refs[5].at[at], 28 + rank, (core, block))
            position += 1
    send(lambda refs: refs[1].at[core], lambda refs: refs[1].at[core], 31, other)
    arrive(lambda refs: refs[1].at[1 - core], 31)
    for copy in sent:
        copy.wait_send()


def scatter_parts(wide, tall):
    buffers = []
    for array in (wide, tall):
        for count in (16, 8, 4, 3, 15):
            buffers.append(pltpu.VMEM((count,) + array.shape[2:], array.dtype))
    return pl.pallas_call(
        scatter_kernel,
        out_shape=(
            jax.ShapeDtypeStruct((2,) + wide.shape[2:], wide.dtype),
            jax.ShapeDtypeStruct((2,) + tall.shape[2:], tall.dtype),
        ),
        in_specs=[pl.BlockSpec(memory_space=pltpu.VMEM)] * 2,
        out_specs=(pl.BlockSpec(memory_space=pltpu.VMEM),) * 2,
        scratch_shapes=buffers
        + [pltpu.SemaphoreType.DMA((2, 32)), pltpu.SemaphoreType.DMA((2, 32))],
        compiler_params=pltpu.CompilerParams(
            collective_id=1, has_side_effects=True, vmem_limit_bytes=52 * 1024 * 1024
        ),
        name="scatter_grads",
    )(wide, tall)


def halves(array, axis):
    size = array.shape[axis] // 2
    return (
        lax.slice_in_dim(array, 0, size, axis=axis),
        lax.slice_in_dim(array, size, 2 * size, axis=axis),
    )


def fill_row(values):
    flat = values.reshape(-1)
    return jnp.pad(flat[None], ((0, 15), (0, 640 - flat.shape[0])))


def gather_all(weights, norm_gains, head_gains):
    query, key, value, out, gate, up, down = weights
    columns = [halves(w, 1) for w in (query, key, value, gate, up)]
    wide = jnp.stack([jnp.concatenate([c[h] for c in columns], axis=1) for h in (0, 1)])
    rows = [halves(w, 0) for w in (out, down)]
    extra = (fill_row(norm_gains), fill_row(head_gains))
    tall = jnp.stack(
        [jnp.concatenate([r[h] for r in rows] + [extra[h]], axis=0) for h in (0, 1)]
    )
    wide, tall = gather_parts(wide, tall)
    wide = wide.reshape(2, 16 * wide.shape[2], wide.shape[3])
    spots = ((0, 512), (512, 640), (640, 768), (768, 1792), (1792, 2816))
    query, key, value, gate, up = (
        jnp.concatenate([wide[0, :, a:b], wide[1, :, a:b]], axis=1) for a, b in spots
    )
    out = jnp.concatenate([tall[0, :, :32], tall[1, :, :32]], axis=1).reshape(1024, 640)
    down = jnp.concatenate([tall[0, :, 32:96], tall[1, :, 32:96]], axis=1).reshape(2048, 640)
    norms = tall[0, :, 96, :160].reshape(16, 4, 40).transpose(1, 0, 2).reshape(4, 640)
    heads = tall[1, :, 96, :32].reshape(16, 2, 16).transpose(1, 0, 2).reshape(2, 256)
    return (query, key, value, out, gate, up, down, norms, heads)


def reduce_all(grads, norm_grad, head_grad):
    low = [g.astype(jnp.bfloat16) for g in grads]
    query, key, value, out, gate, up, down = low
    columns = [halves(w, 1) for w in (query, key, value, gate, up)]
    wide = jnp.stack([jnp.concatenate([c[h] for c in columns], axis=1) for h in (0, 1)])
    wide = wide.reshape(2, 16, 40, 2816)
    norm_low = norm_grad.astype(jnp.bfloat16).reshape(4, 16, 40).transpose(1, 0, 2).reshape(16, 160)
    head_low = head_grad.astype(jnp.bfloat16).reshape(2, 16, 16).transpose(1, 0, 2).reshape(16, 32)
    extra = (
        jnp.pad(norm_low[:, None], ((0, 0), (0, 15), (0, 480))),
        jnp.pad(head_low[:, None], ((0, 0), (0, 15), (0, 608))),
    )
    out = out.reshape(16, 64, 640)
    down = down.reshape(16, 128, 640)
    rows = [halves(w, 1) for w in (out, down)]
    tall = jnp.stack(
        [jnp.concatenate([r[h] for r in rows] + [extra[h]], axis=1) for h in (0, 1)]
    )
    wide, tall = scatter_parts(wide, tall)
    wide = wide.astype(jnp.float32)
    tall = tall.astype(jnp.float32)
    spots = ((0, 512), (512, 640), (640, 768), (768, 1792), (1792, 2816))
    query, key, value, gate, up = (
        jnp.concatenate([wide[0, :, a:b], wide[1, :, a:b]], axis=1) for a, b in spots
    )
    out = jnp.concatenate([tall[0, :32], tall[1, :32]], axis=0)
    down = jnp.concatenate([tall[0, 32:96], tall[1, 32:96]], axis=0)
    norms = tall[0, 96, :160].reshape(4, 40)
    heads = tall[1, 96, :32].reshape(2, 16)
    return (query, key, value, out, gate, up, down, norms, heads)


def gather_plain(weights, norm_gains, head_gains):
    full = tuple(lax.all_gather(w, "shard", axis=0, tiled=True) for w in weights)
    gains = tuple(
        lax.all_gather(g, "shard", axis=1, tiled=True) for g in (norm_gains, head_gains)
    )
    return full + gains


def reduce_plain(grads, norm_grad, head_grad):
    summed = tuple(
        lax.psum(lax.psum_scatter(g, "shard", scatter_dimension=0, tiled=True), "rep")
        for g in grads
    )
    gains = tuple(
        lax.psum(lax.psum_scatter(g, "shard", scatter_dimension=1, tiled=True), "rep")
        for g in (norm_grad, head_grad)
    )
    return summed + gains


def local(
    gather,
    reduce,
    tokens,
    lengths,
    w_query,
    w_key,
    w_value,
    w_out,
    w_gate,
    w_up,
    w_down,
    norm_gains,
    head_gains,
    cotangent,
):
    local_rows = tokens.shape[0]
    row_index = jnp.arange(local_rows, dtype=jnp.int32)
    segment, position = layout(lengths[0], row_index)
    live_mask = (segment < 2).astype(jnp.float32)
    cos_part, sin_part = angles(position, HD)
    gathered = gather(
        (w_query, w_key, w_value, w_out, w_gate, w_up, w_down), norm_gains, head_gains
    )
    (
        full_query,
        full_key,
        full_value,
        full_out,
        full_gate,
        full_up,
        full_down,
        full_norms,
        full_heads,
    ) = gathered
    gains = full_norms.astype(jnp.float32)
    head_scale = full_heads.astype(jnp.float32)
    token_f32 = tokens.astype(jnp.float32)
    normed_in, input_back = jax.vjp(rms_norm, token_f32, gains[0])
    input_low = normed_in.astype(jnp.bfloat16)
    query_raw = jnp.dot(input_low, full_query, preferred_element_type=jnp.float32)
    key_raw = jnp.dot(input_low, full_key, preferred_element_type=jnp.float32)
    value_low = jnp.dot(input_low, full_value, preferred_element_type=jnp.float32).astype(
        jnp.bfloat16
    )
    (query_rot, key_rot), heads_back = jax.vjp(
        partial(prepare_heads, cos_part, sin_part), query_raw, key_raw, head_scale[0], head_scale[1]
    )
    query_low = query_rot.astype(jnp.bfloat16)
    key_low = key_rot.astype(jnp.bfloat16)
    query_rows = query_low.transpose(1, 0, 2).reshape(HQ * local_rows, HD)
    scores = tail_dot(query_rows, key_low).reshape(HQ, local_rows, local_rows)
    scores = jnp.where(causal_mask(segment, row_index)[None], scores, -1e30)
    expo = jnp.exp(scores - jnp.max(scores, axis=-1, keepdims=True))
    probs = (expo / jnp.sum(expo, axis=-1, keepdims=True)).reshape(HQ * local_rows, local_rows)
    probs_low = probs.astype(jnp.bfloat16)
    outputs = jnp.dot(probs_low, value_low, preferred_element_type=jnp.float32)
    attn_low = (
        outputs.astype(jnp.bfloat16)
        .reshape(HQ, local_rows, HD)
        .transpose(1, 0, 2)
        .reshape(local_rows, HQ * HD)
    )
    attn_proj = jnp.dot(attn_low, full_out, preferred_element_type=jnp.float32)
    (resid, normed_mid), mid_back = jax.vjp(middle, token_f32, attn_proj, gains[1], gains[2])
    mid_low = normed_mid.astype(jnp.bfloat16)
    gate_pre = jnp.dot(mid_low, full_gate, preferred_element_type=jnp.float32)
    up_pre = jnp.dot(mid_low, full_up, preferred_element_type=jnp.float32)
    activated, glu_back = jax.vjp(geglu, gate_pre, up_pre)
    act_low = activated.astype(jnp.bfloat16)
    down_out = jnp.dot(act_low, full_down, preferred_element_type=jnp.float32)
    final, tail_back = jax.vjp(partial(finish, live_mask), resid, down_out, gains[3])
    mixed = final.astype(jnp.bfloat16)
    resid_grad, down_grad, final_gain_grad = tail_back(cotangent.astype(jnp.float32))
    down_low = down_grad.astype(jnp.bfloat16)
    grad_down = lead_dot(act_low, down_low)
    act_grad = tail_dot(down_low, full_down)
    gate_grad, up_grad = glu_back(act_grad)
    gate_low = gate_grad.astype(jnp.bfloat16)
    up_low = up_grad.astype(jnp.bfloat16)
    grad_gate = lead_dot(mid_low, gate_low)
    grad_up = lead_dot(mid_low, up_low)
    mid_grad = tail_dot(gate_low, full_gate) + tail_dot(up_low, full_up)
    token_grad_mid, attn_grad, post_gain_grad, pre_gain_grad = mid_back((resid_grad, mid_grad))
    attn_grad_low = attn_grad.astype(jnp.bfloat16)
    grad_out = lead_dot(attn_low, attn_grad_low)
    heads_grad = (
        tail_dot(attn_grad_low, full_out)
        .astype(jnp.bfloat16)
        .reshape(local_rows, HQ, HD)
        .transpose(1, 0, 2)
        .reshape(HQ * local_rows, HD)
    )
    value_grad = lead_dot(probs_low, heads_grad)
    prob_grad = tail_dot(heads_grad, value_low)
    score_grad = (probs * (prob_grad - jnp.sum(probs * prob_grad, axis=-1, keepdims=True))).astype(
        jnp.bfloat16
    )
    query_grad = jnp.dot(score_grad, key_low, preferred_element_type=jnp.float32)
    key_grad = lead_dot(score_grad, query_rows)
    query_grad = query_grad.reshape(HQ, local_rows, HD).transpose(1, 0, 2)
    query_raw_grad, key_raw_grad, query_gain_grad, key_gain_grad = heads_back(
        (query_grad, key_grad)
    )
    query_low_grad = query_raw_grad.astype(jnp.bfloat16)
    key_low_grad = key_raw_grad.astype(jnp.bfloat16)
    value_low_grad = value_grad.astype(jnp.bfloat16)
    grad_query = lead_dot(input_low, query_low_grad)
    grad_key = lead_dot(input_low, key_low_grad)
    grad_value = lead_dot(input_low, value_low_grad)
    input_grad = (
        tail_dot(query_low_grad, full_query)
        + tail_dot(key_low_grad, full_key)
        + tail_dot(value_low_grad, full_value)
    )
    token_grad_in, in_gain_grad = input_back(input_grad)
    tokens_grad = (token_grad_mid + token_grad_in).astype(jnp.bfloat16)
    norm_grad = jnp.stack([in_gain_grad, post_gain_grad, pre_gain_grad, final_gain_grad])
    head_grad = jnp.stack([query_gain_grad, key_gain_grad])
    results = reduce(
        (grad_query, grad_key, grad_value, grad_out, grad_gate, grad_up, grad_down),
        norm_grad,
        head_grad,
    )
    return (
        mixed,
        tokens_grad,
        results[0],
        results[1],
        results[2],
        results[3],
        results[4],
        results[5],
        results[6],
        results[7],
        results[8],
    )


def solution(mesh):
    if mesh.shape["rep"] == 2 and mesh.shape["shard"] == 16:
        steps = (gather_all, reduce_all)
    else:
        steps = (gather_plain, reduce_plain)
    placed = (
        P(("rep", "shard"), None),
        P(("rep", "shard"), None),
        P("shard", None),
        P("shard", None),
        P("shard", None),
        P("shard", None),
        P("shard", None),
        P("shard", None),
        P("shard", None),
        P(None, "shard"),
        P(None, "shard"),
        P(("rep", "shard"), None),
    )
    return jax.shard_map(
        partial(local, *steps),
        mesh=mesh,
        in_specs=placed,
        out_specs=(
            P(("rep", "shard"), None),
            P(("rep", "shard"), None),
            P("shard", None),
            P("shard", None),
            P("shard", None),
            P("shard", None),
            P("shard", None),
            P("shard", None),
            P("shard", None),
            P(None, "shard"),
            P(None, "shard"),
        ),
        check_vma=False,
    )
```

time: 1180 us -> 272 us (0.23)
  waiting for transfers between devices: 866 us -> 0 us
  blocking collectives: 211 us -> 0 us
  Pallas kernels: 0 us -> 168 us
  local copies, waits for them, and re-layouts: 15.8 us -> 44.9 us
  matrix products: 39.4 us -> 22.5 us
  between operations: 17.5 us -> 3.43 us
    reduce_scatter x10 -> x0, waiting for transfers between devices: 595 us -> none  [the longest x1 128 us: local(): lax.psum_scatter(grad_down, 'shard', scatter_dimension=0, tiled=True)]
    all_gather x5 -> x0, waiting for transfers between devices: 174 us -> none  [the longest x1 63.2 us: local(): lax.all_gather(w_up, 'shard', axis=0, tiled=True)]
    pallas_call x0 -> x2, Pallas kernels: none -> 168 us  [the longest x1 88.1 us: scatter_parts(): pl.pallas_call(scatter_kernel, out_shape=(jax.ShapeDtypeStruct((2,) + wid...]
    all_gather x11 -> x0, blocking collectives: 135 us -> none  [the longest x1 32.7 us: local(): lax.all_gather(w_key, 'shard', axis=0, tiled=True)]
    unnamed x25 -> x0, waiting for transfers between devices: 97.6 us -> none
    unnamed x1 -> x0, blocking collectives: 61 us -> none
    psum x1 -> x0, blocking collectives: 15.1 us -> none  [local(): gain_sums = lax.psum((summed[7], summed[8]), 'rep')]
    another operation x2 -> x8, other arithmetic: 0.03 us -> 12.9 us  [the longest x1 6.71 us: reduce_all(): jnp.stack([jnp.concatenate([c[h] for c in columns], axis=1) for h in (0,...]
  transfers between devices with their start and end apart: 20 -> 0, of which waited for: 18 -> 0; matrix products, arithmetic and copies ran while one was open for 5% -> 0% of each run, Pallas kernels for 0% -> 0%
where the time goes in v1:
time: 272 us; the launch traced here: 271 us
  Pallas kernels  168 us (62%)
  local copies, waits for them, and re-layouts  44.9 us (17%)
  other arithmetic  32.1 us (12%)
  matrix products  22.5 us (8%)
  between operations  3.43 us (1%)
    pallas_call x1, Pallas kernels, scatter_parts(): pl.pallas_call(scatter_kernel, out_shape=(jax.ShapeDtypeStruct((2,) + wid...  88.1 us
    pallas_call x1, Pallas kernels, gather_parts(): pl.pallas_call(gather_kernel, out_shape=(jax.ShapeDtypeStruct((2, 16) + w...  80.2 us
    unnamed x174, local copies, waits for them, and re-layouts  19 us
    dot_general x8, matrix products, tail_dot(): lax.dot_general(left, right, (((1,), (1,)), ((), ())), preferred_element_...  10.5 us
    another operation x1, other arithmetic, reduce_all(): jnp.stack([jnp.concatenate([c[h] for c in columns], axis=1) for h in (0,...  6.71 us
    dot_general x9, matrix products, lead_dot(): lax.dot_general(left, right, (((0,), (0,)), ((), ())), preferred_element_...  5.87 us
    squeeze x3, local copies, waits for them, and re-layouts, gather_all(): wide[0, :, a:b]  5.78 us

profile of v1, /device:TPU:9, one launch (start us, length us, event | category | flops | bytes accessed | tf_op | source)
XLA Modules:
  0.0 271.2 jit_solution(18382133713827448873)
XLA Ops:
  0.6 0.8 constant_dynamic-update-slice_fusion.2
  2.9 0.9 slice_dynamic-update-slice_fusion.9
  3.9 1.0 slice_dynamic-update-slice_fusion.8
  4.8 0.8 pad_maximum_fusion.15.wide_in
  5.7 0.8 broadcast_in_dim_reshape.12
  6.4 0.9 fusion.101
  7.4 0.8 fusion.102
  9.0 0.7 pad_maximum_fusion.21.tall_in
  9.7 80.2 %gather_weights.1 = (bf16[2,16,40,2816]{3,2,1,0:T(8,128)(2,1)}, bf16[2,16,112,640]{3,2,1,0:T(8,128)(2,1)}) custom-call(bf16[2,40,2816]{2,1,0:T(8,128)(2,1)} %pad_maximum_fusion.15.wide_in, bf16[2,112,640]{2,1,0:T(8,128)(2,1)} %pad_maximum_fusion.21.tall_in), custom_call_target="tpu_custom_call" | custom-call | tf_op jit(solution)/shard_map/gather_weights/pallas_call | solution.py:191
  89.9 0.9 convert_reduce_fusion
  91.6 1.2 slice_bitcast_fusion.19
  93.4 1.4 slice_bitcast_fusion.7
  94.8 0.8 copy-done.23
  96.0 0.8 convert_reduce_fusion.1
  103.4 1.4 slice_bitcast_fusion.9
  106.4 3.2 %slice_bitcast_fusion.3 = (bf16[640,1024]{1,0:T(8,128)(2,1)S(1)}, bf16[640,1024]{1,0:T(8,128)(2,1)S(1)}, bf16[640,1024]{1,0:T(8,128)(2,1)S(1)}, bf16[640,1024]{1,0:T(8,128)(2,1)S(1)}) fusion(bf16[2,640,2816]{2,1,0:T(8,128)(2,1)} %bitcast.171), kind=kLoop, calls=%fused_computation.31 | loop fusion | bytes 10485760 | tf_op jit(solution)/shard_map/squeeze | solution.py:346
  110.7 1.8 multiply_convert_fusion.1
  113.3 1.3 slice-done.1
  115.3 1.5 copy-done
  117.4 1.2 compare_convert_fusion
  119.2 0.8 mul.581
  120.0 2.4 multiply_reduce_fusion.2
  122.9 3.9 %fusion.21 = (bf16[128,2048]{1,0:T(8,128)(2,1)S(1)}, bf16[128,2048]{1,0:T(8,128)(2,1)S(1)}) fusion(f32[128,2048]{1,0:T(8,128)} %copy-done.79, f32[128,2048]{1,0:T(8,128)} %get-tuple-element.118, bf16[2048,640]{1,0:T(8,128)(2,1)} %bitcast.164, f32[128,640]{1,0:T(8,128)S(1)} %get-tuple-element.120, bf16[128,640]{1,0:T(8,128)(2,1)} %param.23, ...), kind=kOutput, calls=%fused_computation.56 | convolution fusion | flops 342491136 | bytes 6262784 | tf_op jit(solution)/shard_map/dot_general | solution.py:61
  126.9 0.9 fusion.7
  128.9 1.6 multiply_reduce_fusion.3
  130.6 1.5 multiply_reduce_fusion.4
  133.0 1.1 fusion.33
  134.7 1.1 multiply_reduce_fusion.11
  136.1 1.0 convolution_multiply_fusion
  138.0 1.9 fusion.22
  141.7 0.8 fusion.35
  143.1 1.2 slice_dynamic-update-slice_fusion.5
  148.1 1.9 convolution_convert_fusion.2
  150.0 1.7 copy.103
  151.7 1.6 constant_dynamic-update-slice_fusion.9
  153.4 1.7 copy.104
  155.1 1.6 constant_dynamic-update-slice_fusion.8
  156.7 1.9 slice_dynamic-update-slice_fusion.3
  158.6 0.9 convolution_convert_fusion.1
  159.5 1.8 slice_dynamic-update-slice_fusion.2
  161.4 6.7 %pad_maximum_fusion.wide_in = bf16[2,16,40,2816]{3,2,1,0:T(8,128)(2,1)} fusion(bf16[1,16,40,2816]{3,2,1,0:T(8,128)(2,1)} %bitcast.173, bf16[1,16,40,2816]{3,2,1,0:T(8,128)(2,1)} %bitcast.174), kind=kLoop, calls=%fused_computation.1 | loop fusion | flops 3604480 | bytes 14417920 | tf_op jit(solution)/shard_map/stack | solution.py:359
  168.4 1.0 convolution_convert_fusion
  169.4 1.4 fusion.97
  172.6 1.5 fusion.4
  174.1 2.6 pad_maximum_fusion.1.tall_in
  176.7 88.1 %scatter_grads.1 = (bf16[2,40,2816]{2,1,0:T(8,128)(2,1)S(1)}, bf16[2,112,640]{2,1,0:T(8,128)(2,1)S(1)}) custom-call(bf16[2,16,40,2816]{3,2,1,0:T(8,128)(2,1)} %pad_maximum_fusion.wide_in, bf16[2,16,112,640]{3,2,1,0:T(8,128)(2,1)} %pad_maximum_fusion.1.tall_in), custom_call_target="tpu_custom_call" | custom-call | tf_op jit(solution)/shard_map/scatter_grads/pallas_call | solution.py:303
  267.6 0.8 pad_maximum_fusion.18
  269.1 0.7 pad_maximum_fusion.20
  (270 shorter events, 31.3 us)
Async XLA Ops:
  3.8 89.1 %copy-start.1 = (bf16[128,640]{1,0:T(8,128)(2,1)S(1)}, bf16[128,640]{1,0:T(8,128)(2,1)}, u32[]{:S(2)}) copy-start(bf16[128,640]{1,0:T(8,128)(2,1)} %param.12) | copy-start | bytes 491524
  92.8 5.4 %copy-start.25 = (bf16[640,128]{1,0:T(8,128)(2,1)}, bf16[640,128]{1,0:T(8,128)(2,1)S(1)}, u32[]{:S(2)}) copy-start(bf16[640,128]{1,0:T(8,128)(2,1)S(1)} %get-tuple-element.44) | copy-start | bytes 491524
  92.8 5.4 %copy-start.27 = (bf16[640,128]{1,0:T(8,128)(2,1)}, bf16[640,128]{1,0:T(8,128)(2,1)S(1)}, u32[]{:S(2)}) copy-start(bf16[640,128]{1,0:T(8,128)(2,1)S(1)} %get-tuple-element.47) | copy-start | bytes 491524
  93.1 5.1 %copy-start.50 = (f32[128]{0:T(128)}, f32[128]{0:T(128)S(1)}, u32[]{:S(2)}) copy-start(f32[128]{0:T(128)S(1)} %fusion.71) | copy-start | bytes 1540
  93.3 9.7 %copy-start.36 = (bf16[128,256]{1,0:T(8,128)(2,1)}, bf16[128,256]{1,0:T(8,128)(2,1)S(1)}, u32[]{:S(2)}) copy-start(bf16[128,256]{1,0:T(8,128)(2,1)S(1)} %convolution_convert_fusion.9) | copy-start | bytes 196612
  96.0 2.7 %copy-start.68 = (s32[1,2]{1,0:T(1,128)S(1)}, s32[1,2]{1,0:T(1,128)}, u32[]{:S(2)}) copy-start(s32[1,2]{1,0:T(1,128)} %param.13) | copy-start | bytes 28
  98.5 6.3 %copy-start.19 = (f32[128,256]{1,0:T(8,128)}, f32[128,256]{1,0:T(8,128)S(1)}, u32[]{:S(2)}) copy-start(f32[128,256]{1,0:T(8,128)S(1)} %get-tuple-element.112) | copy-start | bytes 393220
  98.5 6.3 %copy-start.77 = (f32[128]{0:T(128)}, f32[128]{0:T(128)S(1)}, u32[]{:S(2)}) copy-start(f32[128]{0:T(128)S(1)} %get-tuple-element.111) | copy-start | bytes 1540
  98.6 2.7 copy-start.46
  98.6 2.7 copy-start.56
  98.8 3.1 %copy-start.63 = (f32[128]{0:T(128)}, f32[128]{0:T(128)S(1)}, u32[]{:S(2)}) copy-start(f32[128]{0:T(128)S(1)} %multiply_exponential_fusion) | copy-start | bytes 1540
  101.7 3.1 %copy-start.41 = (bf16[128,128]{1,0:T(8,128)(2,1)}, bf16[128,128]{1,0:T(8,128)(2,1)S(1)}, u32[]{:S(2)}) copy-start(bf16[128,128]{1,0:T(8,128)(2,1)S(1)} %get-tuple-element.98) | copy-start | bytes 98308
  102.3 2.6 copy-start.21
  106.3 3.3 %copy-start.65 = (f32[128]{0:T(128)}, f32[128]{0:T(128)S(1)}, u32[]{:S(2)}) copy-start(f32[128]{0:T(128)S(1)} %fusion.74) | copy-start | bytes 1540
  106.4 4.3 %copy-start.5 = (bf16[128,640]{1,0:T(8,128)(2,1)}, bf16[128,640]{1,0:T(8,128)(2,1)S(1)}, u32[]{:S(2)}) copy-start(bf16[128,640]{1,0:T(8,128)(2,1)S(1)} %multiply_convert_fusion.3) | copy-start | bytes 491524
  106.4 6.9 %slice-start = ((s8[4587520]{0:T(1024)(128)(4,1)}), s8[393216]{0:T(1024)(128)(4,1)S(1)}, s32[]{:S(2)}) async-start(s8[4587520]{0:T(1024)(128)(4,1)} %bitcast.177), calls=%async_computation | async-start | bytes 786432
  109.6 2.9 %copy-start.13 = (bf16[640,1024]{1,0:T(8,128)(2,1)}, bf16[640,1024]{1,0:T(8,128)(2,1)S(1)}, u32[]{:S(2)}) copy-start(bf16[640,1024]{1,0:T(8,128)(2,1)S(1)} %get-tuple-element.43) | copy-start | bytes 3932164
  109.6 2.9 %copy-start.15 = (bf16[640,1024]{1,0:T(8,128)(2,1)}, bf16[640,1024]{1,0:T(8,128)(2,1)S(1)}, u32[]{:S(2)}) copy-start(bf16[640,1024]{1,0:T(8,128)(2,1)S(1)} %get-tuple-element.41) | copy-start | bytes 3932164
  109.6 3.1 %copy-start.17 = (bf16[640,1024]{1,0:T(8,128)(2,1)}, bf16[640,1024]{1,0:T(8,128)(2,1)S(1)}, u32[]{:S(2)}) copy-start(bf16[640,1024]{1,0:T(8,128)(2,1)S(1)} %get-tuple-element.42) | copy-start | bytes 3932164
  109.6 4.9 %slice-start.1 = ((s8[4587520]{0:T(1024)(128)(4,1)}), s8[4194304]{0:T(1024)(128)(4,1)S(1)}, s32[]{:S(2)}) async-start(s8[4587520]{0:T(1024)(128)(4,1)} %bitcast.177), calls=%async_computation.1 | async-start | bytes 8388608
  110.2 3.0 %copy-start.79 = (f32[128,2048]{1,0:T(8,128)}, f32[128,2048]{1,0:T(8,128)S(1)}, u32[]{:S(2)}) copy-start(f32[128,2048]{1,0:T(8,128)S(1)} %fusion.10) | copy-start | bytes 3145732
  122.9 3.9 %copy-start.71 = (f32[128]{0:T(128)}, f32[128]{0:T(128)S(1)}, u32[]{:S(2)}) copy-start(f32[128]{0:T(128)S(1)} %multiply_multiply_fusion.9) | copy-start | bytes 1540
  122.9 3.9 %copy-start.16 = (bf16[640,1024]{1,0:T(8,128)(2,1)S(1)}, bf16[640,1024]{1,0:T(8,128)(2,1)}, u32[]{:S(2)}) copy-start(bf16[640,1024]{1,0:T(8,128)(2,1)} %copy-done.15) | copy-start | bytes 3932164
  122.9 3.9 %copy-start.18 = (bf16[640,1024]{1,0:T(8,128)(2,1)S(1)}, bf16[640,1024]{1,0:T(8,128)(2,1)}, u32[]{:S(2)}) copy-start(bf16[640,1024]{1,0:T(8,128)(2,1)} %copy-done.17) | copy-start | bytes 3932164
  133.0 4.1 %copy-start.30 = (f32[128,128]{1,0:T(8,128)S(1)}, f32[128,128]{1,0:T(8,128)}, u32[]{:S(2)}) copy-start(f32[128,128]{1,0:T(8,128)} %copy-done.29) | copy-start | bytes 196612
  133.0 4.1 %copy-start.32 = (f32[128,128]{1,0:T(8,128)S(1)}, f32[128,128]{1,0:T(8,128)}, u32[]{:S(2)}) copy-start(f32[128,128]{1,0:T(8,128)} %copy-done.31) | copy-start | bytes 196612
  134.1 3.0 %copy-start.9 = (bf16[128,640]{1,0:T(8,128)(2,1)}, bf16[128,640]{1,0:T(8,128)(2,1)S(1)}, u32[]{:S(2)}) copy-start(bf16[128,640]{1,0:T(8,128)(2,1)S(1)} %fusion.33) | copy-start | bytes 491524
  134.1 3.0 %copy-start.43 = (f32[128,4]{0,1:T(4,128)S(1)}, f32[128,4]{0,1:T(4,128)}, u32[]{:S(2)}) copy-start(f32[128,4]{0,1:T(4,128)} %copy-done.42) | copy-start | bytes 6148
  134.1 3.0 %copy-start.49 = (f32[256]{0:T(256)S(1)}, f32[256]{0:T(256)}, u32[]{:S(2)}) copy-start(f32[256]{0:T(256)} %copy-done.48) | copy-start | bytes 3076
  134.7 2.8 %copy-start.45 = (f32[128,4]{0,1:T(4,128)S(1)}, f32[128,4]{0,1:T(4,128)}, u32[]{:S(2)}) copy-start(f32[128,4]{0,1:T(4,128)} %copy-done.44) | copy-start | bytes 6148
  137.2 2.7 copy-start.22
  137.4 2.6 copy-start.61
  137.4 2.6 copy-start.64
  137.5 3.0 %copy-start.20 = (f32[128,256]{1,0:T(8,128)S(1)}, f32[128,256]{1,0:T(8,128)}, u32[]{:S(2)}) copy-start(f32[128,256]{1,0:T(8,128)} %copy-done.19) | copy-start | bytes 393220
  137.5 3.0 %copy-start.47 = (f32[256]{0:T(256)S(1)}, f32[256]{0:T(256)}, u32[]{:S(2)}) copy-start(f32[256]{0:T(256)} %copy-done.46) | copy-start | bytes 3076
  137.5 3.0 %copy-start.57 = (f32[128]{0:T(128)S(1)}, f32[128]{0:T(128)}, u32[]{:S(2)}) copy-start(f32[128]{0:T(128)} %copy-done.56) | copy-start | bytes 1540
  137.5 3.1 %copy-start.78 = (f32[128]{0:T(128)S(1)}, f32[128]{0:T(128)}, u32[]{:S(2)}) copy-start(f32[128]{0:T(128)} %copy-done.77) | copy-start | bytes 1540
  137.5 3.2 %copy-start.26 = (bf16[640,128]{1,0:T(8,128)(2,1)S(1)}, bf16[640,128]{1,0:T(8,128)(2,1)}, u32[]{:S(2)}) copy-start(bf16[640,128]{1,0:T(8,128)(2,1)} %copy-done.25) | copy-start | bytes 491524
  137.8 3.0 %copy-start.28 = (bf16[640,128]{1,0:T(8,128)(2,1)S(1)}, bf16[640,128]{1,0:T(8,128)(2,1)}, u32[]{:S(2)}) copy-start(bf16[640,128]{1,0:T(8,128)(2,1)} %copy-done.27) | copy-start | bytes 491524
  137.9 3.3 %copy-start.38 = (bf16[640,128]{1,0:T(8,128)(2,1)S(1)}, bf16[640,128]{1,0:T(8,128)(2,1)}, u32[]{:S(2)}) copy-start(bf16[640,128]{1,0:T(8,128)(2,1)} %copy-done.37) | copy-start | bytes 491524
  138.0 3.3 %copy-start.40 = (bf16[640,128]{1,0:T(8,128)(2,1)S(1)}, bf16[640,128]{1,0:T(8,128)(2,1)}, u32[]{:S(2)}) copy-start(bf16[640,128]{1,0:T(8,128)(2,1)} %copy-done.39) | copy-start | bytes 491524
  138.0 3.3 %copy-start.51 = (f32[128]{0:T(128)S(1)}, f32[128]{0:T(128)}, u32[]{:S(2)}) copy-start(f32[128]{0:T(128)} %copy-done.50) | copy-start | bytes 1540
  143.1 5.0 %copy-start.6 = (bf16[128,640]{1,0:T(8,128)(2,1)S(1)}, bf16[128,640]{1,0:T(8,128)(2,1)}, u32[]{:S(2)}) copy-start(bf16[128,640]{1,0:T(8,128)(2,1)} %copy-done.5) | copy-start | bytes 491524
  161.3 7.0 %copy-start.4 = (bf16[128,2048]{1,0:T(8,128)(2,1)S(1)}, bf16[128,2048]{1,0:T(8,128)(2,1)}, u32[]{:S(2)}) copy-start(bf16[128,2048]{1,0:T(8,128)(2,1)} %copy-done.3) | copy-start | bytes 1572868
  161.3 7.0 %copy-start.8 = (bf16[128,640]{1,0:T(8,128)(2,1)S(1)}, bf16[128,640]{1,0:T(8,128)(2,1)}, u32[]{:S(2)}) copy-start(bf16[128,640]{1,0:T(8,128)(2,1)} %param.23) | copy-start | bytes 491524
  161.3 7.0 %copy-start.55 = (f32[128]{0:T(128)S(1)}, f32[128]{0:T(128)}, u32[]{:S(2)}) copy-start(f32[128]{0:T(128)} %compare_convert_fusion) | copy-start | bytes 1540
  161.3 7.0 %copy-start.62 = (f32[128]{0:T(128)S(1)}, f32[128]{0:T(128)}, u32[]{:S(2)}) copy-start(f32[128]{0:T(128)} %fusion.75) | copy-start | bytes 1540
  161.3 7.0 %copy-start.72 = (f32[128]{0:T(128)S(1)}, f32[128]{0:T(128)}, u32[]{:S(2)}) copy-start(f32[128]{0:T(128)} %copy-done.71) | copy-start | bytes 1540
  (34 other events, 43.2 us)

commit v2 on v1

--- a/solution.py
+++ b/solution.py
@@ -63,6 +63,16 @@
     )
 
 
+def double_dot(left, right_pair):
+    left_pair = jnp.stack([left, left])
+    return lax.dot_general(
+        left_pair,
+        jnp.stack([right_pair[0], right_pair[1]]),
+        (((1,), (1,)), ((0,), (0,))),
+        preferred_element_type=jnp.float32,
+    ).astype(jnp.bfloat16)
+
+
 def prepare_heads(cos_part, sin_part, query_raw, key_raw, query_gain, key_gain):
     query_heads = query_raw.reshape(query_raw.shape[0], HQ, HD)
     query_rot = (
@@ -119,10 +129,12 @@
     pl.semaphore_wait(barrier, len(partners))
 
 
-def gather_kernel(wide_in, tall_in, wide_out, tall_out, local_sem, send_sem, recv_sem):
+def gather_kernel(*refs):
+    local_sem, send_sem, recv_sem = refs[-3:]
+    count = (len(refs) - 3) // 2
     core, me, index = place()
     greet(core, me, index)
-    pairs = ((wide_in, wide_out), (tall_in, tall_out))
+    pairs = tuple(zip(refs[:count], refs[count : 2 * count]))
     sent = []
     slot = [0]
 
@@ -187,33 +199,31 @@
         copy.wait_send()
 
 
-def gather_parts(wide, tall):
+def gather_parts(*arrays):
+    count = len(arrays)
     return pl.pallas_call(
         gather_kernel,
-        out_shape=(
-            jax.ShapeDtypeStruct((2, 16) + wide.shape[1:], wide.dtype),
-            jax.ShapeDtypeStruct((2, 16) + tall.shape[1:], tall.dtype),
-        ),
-        in_specs=[pl.BlockSpec(memory_space=pl.ANY)] * 2,
-        out_specs=(pl.BlockSpec(memory_space=pl.ANY),) * 2,
+        out_shape=tuple(jax.ShapeDtypeStruct((2, 16) + a.shape[1:], a.dtype) for a in arrays),
+        in_specs=[pl.BlockSpec(memory_space=pl.ANY)] * count,
+        out_specs=(pl.BlockSpec(memory_space=pl.ANY),) * count,
         scratch_shapes=[
-            pltpu.SemaphoreType.DMA((2, 2)),
-            pltpu.SemaphoreType.DMA((2, 30)),
-            pltpu.SemaphoreType.DMA((2, 2, 16)),
+            pltpu.SemaphoreType.DMA((count, 2)),
+            pltpu.SemaphoreType.DMA((count, 30)),
+            pltpu.SemaphoreType.DMA((count, 2, 16)),
         ],
         compiler_params=pltpu.CompilerParams(collective_id=0, has_side_effects=True),
         name="gather_weights",
-    )(wide, tall)
-
-
-def scatter_kernel(wide_in, tall_in, wide_out, tall_out, *scratch):
+    )(*arrays)
+
+
+def scatter_kernel(*refs):
     core, me, index = place()
-    wide_buffers, tall_buffers = scratch[0:5], scratch[5:10]
-    send_sem, recv_sem = scratch[10:12]
+    send_sem, recv_sem = refs[-2:]
+    count = (len(refs) - 2) // 7
+    scratch = refs[2 * count : -2]
     greet(core, me, index)
-    arrays = (
-        (wide_in, wide_out) + tuple(wide_buffers),
-        (tall_in, tall_out) + tuple(tall_buffers),
+    arrays = tuple(
+        (refs[n], refs[count + n]) + tuple(scratch[5 * n : 5 * n + 5]) for n in range(count)
     )
     sent = []
     slot = [0]
@@ -246,7 +256,7 @@
 
     order = (2, 1, 3, 0)
     position = 0
-    for turned, straight in ((1, 0), (1, 1), (0, 1), (0, 0)):
+    for turned, straight in ((1, 1), (1, 0), (0, 1), (0, 0)):
         for dz in order:
             block = index(dz, turned, straight)
             send(
@@ -258,12 +268,12 @@
             position += 1
 
     position = 0
-    for group, (turned, straight) in enumerate(((0, 1), (1, 1), (1, 0), (0, 0))):
+    for group, (turned, straight) in enumerate(((1, 1), (0, 1), (1, 0), (0, 0))):
         for rank, dz in enumerate(order):
             block = index(dz, turned, straight)
             incoming = [(2, position)]
             if group >= 2:
-                incoming.append((3, {2: 4, 3: 0}[group] + rank))
+                incoming.append((3, (group - 2) * 4 + rank))
             if group == 3:
                 incoming.append((4, rank))
             bases = {2: 0, 3: 16, 4: 24, 5: 28}
@@ -295,106 +305,111 @@
         copy.wait_send()
 
 
-def scatter_parts(wide, tall):
+def scatter_parts(*arrays):
+    count = len(arrays)
     buffers = []
-    for array in (wide, tall):
-        for count in (16, 8, 4, 3, 15):
-            buffers.append(pltpu.VMEM((count,) + array.shape[2:], array.dtype))
+    for array in arrays:
+        for slots in (16, 8, 4, 3, 15):
+            buffers.append(pltpu.VMEM((slots,) + array.shape[2:], array.dtype))
     return pl.pallas_call(
         scatter_kernel,
-        out_shape=(
-            jax.ShapeDtypeStruct((2,) + wide.shape[2:], wide.dtype),
-            jax.ShapeDtypeStruct((2,) + tall.shape[2:], tall.dtype),
-        ),
-        in_specs=[pl.BlockSpec(memory_space=pltpu.VMEM)] * 2,
-        out_specs=(pl.BlockSpec(memory_space=pltpu.VMEM),) * 2,
+        out_shape=tuple(jax.ShapeDtypeStruct((2,) + a.shape[2:], a.dtype) for a in arrays),
+        in_specs=[pl.BlockSpec(memory_space=pltpu.VMEM)] * count,
+        out_specs=(pl.BlockSpec(memory_space=pltpu.VMEM),) * count,
         scratch_shapes=buffers
-        + [pltpu.SemaphoreType.DMA((2, 32)), pltpu.SemaphoreType.DMA((2, 32))],
+        + [pltpu.SemaphoreType.DMA((count, 32)), pltpu.SemaphoreType.DMA((count, 32))],
         compiler_params=pltpu.CompilerParams(
             collective_id=1, has_side_effects=True, vmem_limit_bytes=52 * 1024 * 1024
         ),
         name="scatter_grads",
-    )(wide, tall)
-
-
-def halves(array, axis):
-    size = array.shape[axis] // 2
-    return (
-        lax.slice_in_dim(array, 0, size, axis=axis),
-        lax.slice_in_dim(array, size, 2 * size, axis=axis),
-    )
-
-
-def fill_row(values):
-    flat = values.reshape(-1)
-    return jnp.pad(flat[None], ((0, 15), (0, 640 - flat.shape[0])))
+    )(*arrays)
+
+
+def pair(*columns):
+    return jnp.stack(
+        [
+            jnp.concatenate(
+                [c[:, h * c.shape[1] // 2 : (h + 1) * c.shape[1] // 2] for c in columns], axis=1
+            )
+            for h in (0, 1)
+        ]
+    )
+
+
+def unpair(both, start, size):
+    return jnp.concatenate(
+        [both[h, :, start : start + size] for h in (0, 1)], axis=1
+    )
 
 
 def gather_all(weights, norm_gains, head_gains):
     query, key, value, out, gate, up, down = weights
-    columns = [halves(w, 1) for w in (query, key, value, gate, up)]
-    wide = jnp.stack([jnp.concatenate([c[h] for c in columns], axis=1) for h in (0, 1)])
-    rows = [halves(w, 0) for w in (out, down)]
-    extra = (fill_row(norm_gains), fill_row(head_gains))
-    tall = jnp.stack(
-        [jnp.concatenate([r[h] for r in rows] + [extra[h]], axis=0) for h in (0, 1)]
-    )
-    wide, tall = gather_parts(wide, tall)
-    wide = wide.reshape(2, 16 * wide.shape[2], wide.shape[3])
-    spots = ((0, 512), (512, 640), (640, 768), (768, 1792), (1792, 2816))
-    query, key, value, gate, up = (
-        jnp.concatenate([wide[0, :, a:b], wide[1, :, a:b]], axis=1) for a, b in spots
-    )
-    out = jnp.concatenate([tall[0, :, :32], tall[1, :, :32]], axis=1).reshape(1024, 640)
-    down = jnp.concatenate([tall[0, :, 32:96], tall[1, :, 32:96]], axis=1).reshape(2048, 640)
-    norms = tall[0, :, 96, :160].reshape(16, 4, 40).transpose(1, 0, 2).reshape(4, 640)
-    heads = tall[1, :, 96, :32].reshape(16, 2, 16).transpose(1, 0, 2).reshape(2, 256)
-    return (query, key, value, out, gate, up, down, norms, heads)
-
-
-def reduce_all(grads, norm_grad, head_grad):
-    low = [g.astype(jnp.bfloat16) for g in grads]
-    query, key, value, out, gate, up, down = low
-    columns = [halves(w, 1) for w in (query, key, value, gate, up)]
-    wide = jnp.stack([jnp.concatenate([c[h] for c in columns], axis=1) for h in (0, 1)])
-    wide = wide.reshape(2, 16, 40, 2816)
-    norm_low = norm_grad.astype(jnp.bfloat16).reshape(4, 16, 40).transpose(1, 0, 2).reshape(16, 160)
-    head_low = head_grad.astype(jnp.bfloat16).reshape(2, 16, 16).transpose(1, 0, 2).reshape(16, 32)
-    extra = (
-        jnp.pad(norm_low[:, None], ((0, 0), (0, 15), (0, 480))),
-        jnp.pad(head_low[:, None], ((0, 0), (0, 15), (0, 608))),
-    )
-    out = out.reshape(16, 64, 640)
-    down = down.reshape(16, 128, 640)
-    rows = [halves(w, 1) for w in (out, down)]
-    tall = jnp.stack(
-        [jnp.concatenate([r[h] for r in rows] + [extra[h]], axis=1) for h in (0, 1)]
-    )
-    wide, tall = scatter_parts(wide, tall)
-    wide = wide.astype(jnp.float32)
-    tall = tall.astype(jnp.float32)
-    spots = ((0, 512), (512, 640), (640, 768), (768, 1792), (1792, 2816))
-    query, key, value, gate, up = (
-        jnp.concatenate([wide[0, :, a:b], wide[1, :, a:b]], axis=1) for a, b in spots
-    )
-    out = jnp.concatenate([tall[0, :32], tall[1, :32]], axis=0)
-    down = jnp.concatenate([tall[0, 32:96], tall[1, 32:96]], axis=0)
-    norms = tall[0, 96, :160].reshape(4, 40)
-    heads = tall[1, 96, :32].reshape(2, 16)
-    return (query, key, value, out, gate, up, down, norms, heads)
+    gains = jnp.pad(norm_gains.T, ((0, 0), (0, 124))) + jnp.pad(
+        head_gains.T, ((0, 24), (4, 122))
+    )
+    front = pair(query, key, value, jnp.concatenate([gains, gains], axis=1))
+    front, wide, tall, high = gather_parts(
+        front, pair(gate, up), out.reshape(2, 32, 640), down.reshape(2, 64, 640)
+    )
+    out = jnp.swapaxes(tall, 0, 1).reshape(1024, 640)
+    down = jnp.swapaxes(high, 0, 1).reshape(2048, 640)
+    norms = front[0, :, :, 768:772].reshape(640, 4).T
+    heads = front[0, :, :16, 772:774].reshape(256, 2).T
+    return (front.reshape(2, 640, 896), out, wide.reshape(2, 640, 2048), down, norms, heads)
 
 
 def gather_plain(weights, norm_gains, head_gains):
-    full = tuple(lax.all_gather(w, "shard", axis=0, tiled=True) for w in weights)
-    gains = tuple(
+    query, key, value, out, gate, up, down = (
+        lax.all_gather(w, "shard", axis=0, tiled=True) for w in weights
+    )
+    norms, heads = (
         lax.all_gather(g, "shard", axis=1, tiled=True) for g in (norm_gains, head_gains)
     )
-    return full + gains
-
-
-def reduce_plain(grads, norm_grad, head_grad):
+    blank = jnp.zeros((query.shape[0], 256), query.dtype)
+    return (pair(query, key, value, blank), out, pair(gate, up), down, norms, heads)
+
+
+def reduce_all(front, out, wide, down, norm_grad, head_grad):
+    gains = jnp.pad(norm_grad.T, ((0, 0), (0, 124))) + jnp.pad(
+        jnp.pad(head_grad.T.reshape(16, 16, 2), ((0, 0), (0, 24), (0, 0))).reshape(640, 2),
+        ((0, 0), (4, 122)),
+    )
+    gains = gains.astype(jnp.bfloat16)
+    front = lax.dynamic_update_slice(front, gains[None], (0, 0, 768))
+    tall = jnp.swapaxes(out.reshape(16, 2, 32, 640), 0, 1)
+    high = jnp.swapaxes(down.reshape(16, 2, 64, 640), 0, 1)
+    summed = scatter_parts(
+        front.reshape(2, 16, 40, 896), tall, wide.reshape(2, 16, 40, 2048), high
+    )
+    front, tall, wide, high = (v.astype(jnp.float32) for v in summed)
+    return (
+        unpair(front, 0, 512),
+        unpair(front, 512, 128),
+        unpair(front, 640, 128),
+        tall.reshape(64, 640),
+        unpair(wide, 0, 1024),
+        unpair(wide, 1024, 1024),
+        high.reshape(128, 640),
+        front[0, :, 768:772].T,
+        front[0, :16, 772:774].T,
+    )
+
+
+def reduce_plain(front, out, wide, down, norm_grad, head_grad):
+    grads = (
+        unpair(front, 0, 512),
+        unpair(front, 512, 128),
+        unpair(front, 640, 128),
+        out,
+        unpair(wide, 0, 1024),
+        unpair(wide, 1024, 1024),
+        down,
+    )
     summed = tuple(
-        lax.psum(lax.psum_scatter(g, "shard", scatter_dimension=0, tiled=True), "rep")
+        lax.psum(
+            lax.psum_scatter(g.astype(jnp.float32), "shard", scatter_dimension=0, tiled=True),
+            "rep",
+        )
         for g in grads
     )
     gains = tuple(
@@ -428,27 +443,16 @@
     gathered = gather(
         (w_query, w_key, w_value, w_out, w_gate, w_up, w_down), norm_gains, head_gains
     )
-    (
-        full_query,
-        full_key,
-        full_value,
-        full_out,
-        full_gate,
-        full_up,
-        full_down,
-        full_norms,
-        full_heads,
-    ) = gathered
+    front, full_out, wide, full_down, full_norms, full_heads = gathered
     gains = full_norms.astype(jnp.float32)
     head_scale = full_heads.astype(jnp.float32)
     token_f32 = tokens.astype(jnp.float32)
     normed_in, input_back = jax.vjp(rms_norm, token_f32, gains[0])
     input_low = normed_in.astype(jnp.bfloat16)
-    query_raw = jnp.dot(input_low, full_query, preferred_element_type=jnp.float32)
-    key_raw = jnp.dot(input_low, full_key, preferred_element_type=jnp.float32)
-    value_low = jnp.dot(input_low, full_value, preferred_element_type=jnp.float32).astype(
-        jnp.bfloat16
-    )
+    raw = [jnp.dot(input_low, front[h], preferred_element_type=jnp.float32) for h in (0, 1)]
+    query_raw = jnp.concatenate([r[:, :512] for r in raw], axis=1)
+    key_raw = jnp.concatenate([r[:, 512:640] for r in raw], axis=1)
+    value_low = jnp.concatenate([r[:, 640:768] for r in raw], axis=1).astype(jnp.bfloat16)
     (query_rot, key_rot), heads_back = jax.vjp(
         partial(prepare_heads, cos_part, sin_part), query_raw, key_raw, head_scale[0], head_scale[1]
     )
@@ -470,26 +474,26 @@
     attn_proj = jnp.dot(attn_low, full_out, preferred_element_type=jnp.float32)
     (resid, normed_mid), mid_back = jax.vjp(middle, token_f32, attn_proj, gains[1], gains[2])
     mid_low = normed_mid.astype(jnp.bfloat16)
-    gate_pre = jnp.dot(mid_low, full_gate, preferred_element_type=jnp.float32)
-    up_pre = jnp.dot(mid_low, full_up, preferred_element_type=jnp.float32)
-    activated, glu_back = jax.vjp(geglu, gate_pre, up_pre)
-    act_low = activated.astype(jnp.bfloat16)
+    pre = [jnp.dot(mid_low, wide[h], preferred_element_type=jnp.float32) for h in (0, 1)]
+    hidden = pre[0].shape[1] // 2
+    glu = [jax.vjp(geglu, p[:, :hidden], p[:, hidden:]) for p in pre]
+    act_low = jnp.concatenate([act.astype(jnp.bfloat16) for act, _ in glu], axis=1)
     down_out = jnp.dot(act_low, full_down, preferred_element_type=jnp.float32)
     final, tail_back = jax.vjp(partial(finish, live_mask), resid, down_out, gains[3])
     mixed = final.astype(jnp.bfloat16)
     resid_grad, down_grad, final_gain_grad = tail_back(cotangent.astype(jnp.float32))
     down_low = down_grad.astype(jnp.bfloat16)
-    grad_down = lead_dot(act_low, down_low)
+    grad_down = lead_dot(act_low, down_low).astype(jnp.bfloat16)
     act_grad = tail_dot(down_low, full_down)
-    gate_grad, up_grad = glu_back(act_grad)
-    gate_low = gate_grad.astype(jnp.bfloat16)
-    up_low = up_grad.astype(jnp.bfloat16)
-    grad_gate = lead_dot(mid_low, gate_low)
-    grad_up = lead_dot(mid_low, up_low)
-    mid_grad = tail_dot(gate_low, full_gate) + tail_dot(up_low, full_up)
+    pre_low = []
+    for h, (_, glu_back) in enumerate(glu):
+        parts = glu_back(act_grad[:, h * hidden : (h + 1) * hidden])
+        pre_low.append(jnp.concatenate([g.astype(jnp.bfloat16) for g in parts], axis=1))
+    grad_wide = double_dot(mid_low, pre_low)
+    mid_grad = tail_dot(pre_low[0], wide[0]) + tail_dot(pre_low[1], wide[1])
     token_grad_mid, attn_grad, post_gain_grad, pre_gain_grad = mid_back((resid_grad, mid_grad))
     attn_grad_low = attn_grad.astype(jnp.bfloat16)
-    grad_out = lead_dot(attn_low, attn_grad_low)
+    grad_out = lead_dot(attn_low, attn_grad_low).astype(jnp.bfloat16)
     heads_grad = (
         tail_dot(attn_grad_low, full_out)
         .astype(jnp.bfloat16)
@@ -511,23 +515,15 @@
     query_low_grad = query_raw_grad.astype(jnp.bfloat16)
     key_low_grad = key_raw_grad.astype(jnp.bfloat16)
     value_low_grad = value_grad.astype(jnp.bfloat16)
-    grad_query = lead_dot(input_low, query_low_grad)
-    grad_key = lead_dot(input_low, key_low_grad)
-    grad_value = lead_dot(input_low, value_low_grad)
-    input_grad = (
-        tail_dot(query_low_grad, full_query)
-        + tail_dot(key_low_grad, full_key)
-        + tail_dot(value_low_grad, full_value)
-    )
+    blank = jnp.zeros((local_rows, 256), jnp.bfloat16)
+    raw_low = pair(query_low_grad, key_low_grad, value_low_grad, blank)
+    grad_front = double_dot(input_low, raw_low)
+    input_grad = tail_dot(raw_low[0], front[0]) + tail_dot(raw_low[1], front[1])
     token_grad_in, in_gain_grad = input_back(input_grad)
     tokens_grad = (token_grad_mid + token_grad_in).astype(jnp.bfloat16)
     norm_grad = jnp.stack([in_gain_grad, post_gain_grad, pre_gain_grad, final_gain_grad])
     head_grad = jnp.stack([query_gain_grad, key_gain_grad])
-    results = reduce(
-        (grad_query, grad_key, grad_value, grad_out, grad_gate, grad_up, grad_down),
-        norm_grad,
-        head_grad,
-    )
+    results = reduce(grad_front, grad_out, grad_wide, grad_down, norm_grad, head_grad)
     return (
         mixed,
         tokens_grad,

time: 272 us -> 251 us (0.923)
  Pallas kernels: 168 us -> 158 us
  other arithmetic: 32.1 us -> 24.3 us
  local copies, waits for them, and re-layouts: 44.9 us -> 41 us
    pallas_call x2, Pallas kernels: 168 us -> 158 us  [the longest x1 79.4 us: gather_parts(): pl.pallas_call(gather_kernel, out_shape=tuple((jax.ShapeDtypeStruct((2, 1...]
    unnamed x174 -> x177, local copies, waits for them, and re-layouts: 19 us -> 9.23 us
    another operation x8 -> x11, other arithmetic: 12.9 us -> 4.51 us  [the longest x5 2.51 us: pair(): jnp.stack([jnp.concatenate([c[:, h * c.shape[1] // 2:(h + 1) * c.shape[1]...]
    slice x12 -> x19, local copies, waits for them, and re-layouts: 8.47 us -> 16.3 us  [the longest x7 6.4 us: pair(): c[:, h * c.shape[1] // 2:(h + 1) * c.shape[1] // 2]]
    squeeze x10 -> x3, local copies, waits for them, and re-layouts: 7.7 us -> 0.06 us  [unpair(): both[h, :, start:start + size]]
    transpose x2 -> x3, local copies, waits for them, and re-layouts: 0.02 us -> 5.26 us  [the longest x1 3.7 us: gather_all(): down = jnp.swapaxes(high, 0, 1).reshape(2048, 640)]
    dot_general x9 -> x4, matrix products: 5.87 us -> 1.87 us  [lead_dot(): lax.dot_general(left, right, (((0,), (0,)), ((), ())), preferred_element_...]
    dot_general x5 -> x6, matrix products: 3.36 us -> 6.81 us  [the longest x2 4.71 us: double_dot(): lax.dot_general(left_pair, jnp.stack([right_pair[0], right_pair[1]]), (((...]
where the time goes in v2:
time: 251 us; the launch traced here: 248 us
  Pallas kernels  158 us (63%)
  local copies, waits for them, and re-layouts  41 us (16%)
  other arithmetic  24.3 us (10%)
  matrix products  21.1 us (8%)
  between operations  3.34 us (1%)
    pallas_call x1, Pallas kernels, gather_parts(): pl.pallas_call(gather_kernel, out_shape=tuple((jax.ShapeDtypeStruct((2, 1...  79.4 us
    pallas_call x1, Pallas kernels, scatter_parts(): pl.pallas_call(scatter_kernel, out_shape=tuple((jax.ShapeDtypeStruct((2,)...  78.8 us
    unnamed x177, local copies, waits for them, and re-layouts  9.23 us
    dot_general x7, matrix products, tail_dot(): lax.dot_general(left, right, (((1,), (1,)), ((), ())), preferred_element_...  7.78 us
    slice x7, local copies, waits for them, and re-layouts, pair(): c[:, h * c.shape[1] // 2:(h + 1) * c.shape[1] // 2]  6.4 us

profile of v2, /device:TPU:9, one launch (start us, length us, event | category | flops | bytes accessed | tf_op | source)
XLA Modules:
  0.0 248.0 jit_solution(14984444391136080092)
XLA Ops:
  2.2 0.8 fusion.115
  3.7 0.8 fusion.112
  5.2 0.9 fusion.111
  6.1 0.9 fusion.110
  7.9 79.4 %gather_weights.1 = (bf16[2,16,40,896]{3,2,1,0:T(8,128)(2,1)}, bf16[2,16,40,2048]{3,2,1,0:T(8,128)(2,1)}, bf16[2,16,32,640]{3,2,1,0:T(8,128)(2,1)}, bf16[2,16,64,640]{3,2,1,0:T(8,128)(2,1)}) custom-call(bf16[2,40,896]{2,1,0:T(8,128)(2,1)} %pad_maximum_fusion.12.refs_0_, bf16[2,40,2048]{2,1,0:T(8,128)(2,1)} %pad_maximum_fusion.8.refs_1_, ...), custom_call_target="tpu_custom_call" | custom-call | tf_op jit(solution)/shard_map/gather_weights/pallas_call | solution.py:204
  87.3 3.7 %copy.128 = bf16[16,2,64,640]{3,2,1,0:T(8,128)(2,1)} copy(bf16[16,2,64,640]{3,2,0,1:T(8,128)(2,1)} %bitcast.193) | data formatting | bytes 5242880 | tf_op jit(solution)/shard_map/transpose | solution.py:355
  91.0 2.0 fusion.107
  93.0 0.9 slice.198
  94.2 1.8 fusion.108
  98.3 0.9 slice.204
  99.4 1.1 reshape.370
  100.5 1.3 multiply_reduce_fusion.1
  102.4 0.8 slice.251
  103.3 0.8 slice.250
  104.4 1.3 fusion.118
  107.5 1.0 fusion.70
  109.9 2.4 fusion.119
  112.3 1.1 broadcast_divide_fusion
  113.4 0.9 slice.339
  114.3 0.9 slice.340
  115.1 0.9 convolution_convert_fusion.5
  116.0 1.8 copy.126
  117.9 1.6 copy.127
  121.0 0.9 copy-done
  122.8 0.9 copy-done.1
  125.0 1.4 multiply_reduce_fusion.2
  126.5 0.9 fusion.105
  127.4 0.8 fusion.20
  128.3 1.0 fusion.32
  129.3 1.6 multiply_reduce_fusion.3
  131.0 1.0 multiply_reduce_fusion.4
  136.5 1.0 multiply_add_fusion.1
  138.3 0.9 fusion.21
  139.2 1.8 copy.134
  141.0 1.7 fusion.109
  142.7 1.0 copy.150
  143.8 1.9 fusion.66
  145.8 1.0 copy.151
  146.8 1.5 fusion.35
  148.5 0.8 fusion.99
  149.3 1.0 fusion.65
  150.4 0.8 convolution_convert_fusion.2
  152.2 0.9 copy.139
  153.1 1.3 fusion.52
  156.1 3.9 %convolution_convert_fusion = bf16[2,640,2048]{2,1,0:T(8,128)(2,1)} fusion(bf16[1,128,2048]{2,1,0:T(8,128)(2,1)S(1)} %fusion.30, bf16[1,128,2048]{2,1,0:T(8,128)(2,1)S(1)} %fusion.31, bf16[1,128,640]{2,1,0:T(8,128)(2,1)S(1)} %fusion.149), kind=kOutput, calls=%fused_computation.1 | convolution fusion | flops 674398208 | bytes 6455296 | tf_op jit(solution)/shard_map/dot_general | solution.py:68
  160.1 1.0 convolution_convert_fusion.1
  161.0 1.8 copy.164
  162.8 78.8 %scatter_grads.1 = (bf16[2,40,896]{2,1,0:T(8,128)(2,1)S(1)}, bf16[2,32,640]{2,1,0:T(8,128)(2,1)S(1)}, bf16[2,40,2048]{2,1,0:T(8,128)(2,1)S(1)}, bf16[2,64,640]{2,1,0:T(8,128)(2,1)S(1)}) custom-call(bf16[2,16,40,896]{3,2,1,0:T(8,128)(2,1)} %bitcast.185, bf16[2,16,32,640]{3,2,1,0:T(8,128)(2,1)S(1)} %bitcast.170, bf16[2,16,40,2048]{3,2,1,0:T(8,128)(2,1)} %bitcast.177, ...), custom_call_target="tpu_custom_call" | custom-call | tf_op jit(solution)/shard_map/scatter_grads/pallas_call | solution.py:314
  (264 shorter events, 26.7 us)
Async XLA Ops:
  87.3 3.7 %copy-start.5 = (bf16[2,16,40,2048]{3,2,1,0:T(8,128)(2,1)S(1)}, bf16[2,16,40,2048]{3,2,1,0:T(8,128)(2,1)}, u32[]{:S(2)}) copy-start(bf16[2,16,40,2048]{3,2,1,0:T(8,128)(2,1)} %get-tuple-element.21) | copy-start | bytes 15728644
  99.4 8.1 %copy-start.56 = (f32[1,256]{1,0:T(1,128)}, f32[1,256]{1,0:T(1,128)S(1)}, u32[]{:S(2)}) copy-start(f32[1,256]{1,0:T(1,128)S(1)} %get-tuple-element.152) | copy-start | bytes 3076
  104.1 8.2 %copy-start.33 = (f32[128,128]{1,0:T(8,128)}, f32[128,128]{1,0:T(8,128)S(1)}, u32[]{:S(2)}) copy-start(f32[128,128]{1,0:T(8,128)S(1)} %slice.250) | copy-start | bytes 196612
  104.2 3.3 %copy-start.84 = (f32[128]{0:T(128)}, f32[128]{0:T(128)S(1)}, u32[]{:S(2)}) copy-start(f32[128]{0:T(128)S(1)} %multiply_reduce_fusion.14) | copy-start | bytes 1540
  104.2 3.2 %copy-start.70 = (f32[128]{0:T(128)}, f32[128]{0:T(128)S(1)}, u32[]{:S(2)}) copy-start(f32[128]{0:T(128)S(1)} %fusion.83) | copy-start | bytes 1540
  104.3 4.1 %copy-start.80 = (f32[128]{0:T(128)}, f32[128]{0:T(128)S(1)}, u32[]{:S(2)}) copy-start(f32[128]{0:T(128)S(1)} %multiply_exponential_fusion) | copy-start | bytes 1540
  109.1 3.1 %copy-start.37 = (bf16[128,4,256]{2,0,1:T(8,128)(2,1)}, bf16[128,4,256]{2,0,1:T(8,128)(2,1)S(1)}, u32[]{:S(2)}) copy-start(bf16[128,4,256]{2,0,1:T(8,128)(2,1)S(1)} %fusion.23) | copy-start | bytes 786436
  113.3 6.6 %copy-start.10 = (f32[4,128,128]{2,1,0:T(8,128)}, f32[4,128,128]{2,1,0:T(8,128)S(1)}, u32[]{:S(2)}) copy-start(f32[4,128,128]{2,1,0:T(8,128)S(1)} %broadcast_divide_fusion) | copy-start | bytes 786436
  114.3 5.7 %copy-start.42 = (bf16[128,128]{1,0:T(8,128)(2,1)}, bf16[128,128]{1,0:T(8,128)(2,1)S(1)}, u32[]{:S(2)}) copy-start(bf16[128,128]{1,0:T(8,128)(2,1)S(1)} %slice.339) | copy-start | bytes 98308
  115.1 4.8 %copy-start.44 = (bf16[128,128]{1,0:T(8,128)(2,1)}, bf16[128,128]{1,0:T(8,128)(2,1)S(1)}, u32[]{:S(2)}) copy-start(bf16[128,128]{1,0:T(8,128)(2,1)S(1)} %slice.340) | copy-start | bytes 98308
  120.2 10.8 %copy-start.63 = (f32[128]{0:T(128)}, f32[128]{0:T(128)S(1)}, u32[]{:S(2)}) copy-start(f32[128]{0:T(128)S(1)} %fusion.85) | copy-start | bytes 1540
  123.7 2.7 %copy-start.21 = (bf16[128,1024]{1,0:T(8,128)(2,1)}, bf16[128,1024]{1,0:T(8,128)(2,1)S(1)}, u32[]{:S(2)}) copy-start(bf16[128,1024]{1,0:T(8,128)(2,1)S(1)} %multiply_convert_fusion.3) | copy-start | bytes 786436
  124.4 3.9 %copy-start.3 = (f32[128,640]{1,0:T(8,128)}, f32[128,640]{1,0:T(8,128)S(1)}, u32[]{:S(2)}) copy-start(f32[128,640]{1,0:T(8,128)S(1)} %get-tuple-element.163) | copy-start | bytes 983044
  125.0 6.0 %copy-start.65 = (f32[128]{0:T(128)}, f32[128]{0:T(128)S(1)}, u32[]{:S(2)}) copy-start(f32[128]{0:T(128)S(1)} %compare_convert_fusion) | copy-start | bytes 1540
  125.0 3.3 %copy-start.68 = (f32[128]{0:T(128)}, f32[128]{0:T(128)S(1)}, u32[]{:S(2)}) copy-start(f32[128]{0:T(128)S(1)} %fusion.86) | copy-start | bytes 1540
  131.0 2.9 %copy-start.43 = (bf16[128,128]{1,0:T(8,128)(2,1)S(1)}, bf16[128,128]{1,0:T(8,128)(2,1)}, u32[]{:S(2)}) copy-start(bf16[128,128]{1,0:T(8,128)(2,1)} %copy-done.42) | copy-start | bytes 98308
  131.0 2.9 %copy-start.45 = (bf16[128,128]{1,0:T(8,128)(2,1)S(1)}, bf16[128,128]{1,0:T(8,128)(2,1)}, u32[]{:S(2)}) copy-start(bf16[128,128]{1,0:T(8,128)(2,1)} %copy-done.44) | copy-start | bytes 98308
  132.2 3.2 %copy-start.85 = (f32[128]{0:T(128)S(1)}, f32[128]{0:T(128)}, u32[]{:S(2)}) copy-start(f32[128]{0:T(128)} %copy-done.84) | copy-start | bytes 1540
  132.8 3.4 %copy-start.46 = (bf16[128,128]{1,0:T(8,128)(2,1)S(1)}, bf16[128,128]{1,0:T(8,128)(2,1)}, u32[]{:S(2)}) copy-start(bf16[128,128]{1,0:T(8,128)(2,1)} %get-tuple-element.136) | copy-start | bytes 98308
  132.8 3.4 %copy-start.47 = (bf16[128,128]{1,0:T(8,128)(2,1)S(1)}, bf16[128,128]{1,0:T(8,128)(2,1)}, u32[]{:S(2)}) copy-start(bf16[128,128]{1,0:T(8,128)(2,1)} %get-tuple-element.137) | copy-start | bytes 98308
  133.8 3.7 %copy-start.53 = (f32[128,4]{0,1:T(4,128)S(1)}, f32[128,4]{0,1:T(4,128)}, u32[]{:S(2)}) copy-start(f32[128,4]{0,1:T(4,128)} %copy-done.52) | copy-start | bytes 6148
  133.8 3.7 %copy-start.62 = (f32[1,256]{1,0:T(1,128)S(1)}, f32[1,256]{1,0:T(1,128)}, u32[]{:S(2)}) copy-start(f32[1,256]{1,0:T(1,128)} %copy-done.61) | copy-start | bytes 3076
  134.1 4.2 %copy-start.55 = (f32[128,4]{0,1:T(4,128)S(1)}, f32[128,4]{0,1:T(4,128)}, u32[]{:S(2)}) copy-start(f32[128,4]{0,1:T(4,128)} %copy-done.54) | copy-start | bytes 6148
  136.4 7.3 %copy-start.9 = (bf16[1,16,40,896]{3,2,1,0:T(8,128)(2,1)S(1)}, bf16[1,16,40,896]{3,2,1,0:T(8,128)(2,1)}, u32[]{:S(2)}) copy-start(bf16[1,16,40,896]{3,2,1,0:T(8,128)(2,1)} %copy-done.8) | copy-start | bytes 3440644
  136.4 7.3 %copy-start.49 = (bf16[128,128]{1,0:T(8,128)(2,1)S(1)}, bf16[128,128]{1,0:T(8,128)(2,1)}, u32[]{:S(2)}) copy-start(bf16[128,128]{1,0:T(8,128)(2,1)} %get-tuple-element.143) | copy-start | bytes 98308
  137.5 9.3 %copy-start.7 = (bf16[1,16,40,896]{3,2,1,0:T(8,128)(2,1)S(1)}, bf16[1,16,40,896]{3,2,1,0:T(8,128)(2,1)}, u32[]{:S(2)}) copy-start(bf16[1,16,40,896]{3,2,1,0:T(8,128)(2,1)} %copy-done.6) | copy-start | bytes 3440644
  137.5 9.3 %copy-start.14 = (bf16[128,640]{1,0:T(8,128)(2,1)S(1)}, bf16[128,640]{1,0:T(8,128)(2,1)}, u32[]{:S(2)}) copy-start(bf16[128,640]{1,0:T(8,128)(2,1)} %param.12) | copy-start | bytes 491524
  137.5 9.3 %copy-start.48 = (bf16[128,128]{1,0:T(8,128)(2,1)S(1)}, bf16[128,128]{1,0:T(8,128)(2,1)}, u32[]{:S(2)}) copy-start(bf16[128,128]{1,0:T(8,128)(2,1)} %get-tuple-element.142) | copy-start | bytes 98308
  141.0 7.4 %copy-start.83 = (f32[128]{0:T(128)S(1)}, f32[128]{0:T(128)}, u32[]{:S(2)}) copy-start(f32[128]{0:T(128)} %copy-done.82) | copy-start | bytes 1540
  141.0 7.4 %copy-start.16 = (f32[128,640]{1,0:T(8,128)S(1)}, f32[128,640]{1,0:T(8,128)}, u32[]{:S(2)}) copy-start(f32[128,640]{1,0:T(8,128)} %copy-done.15) | copy-start | bytes 983044
  141.0 7.4 %copy-start.75 = (f32[128]{0:T(128)S(1)}, f32[128]{0:T(128)}, u32[]{:S(2)}) copy-start(f32[128]{0:T(128)} %copy-done.74) | copy-start | bytes 1540
  143.7 5.6 %copy-start.41 = (bf16[128,512]{1,0:T(8,128)(2,1)}, bf16[128,512]{1,0:T(8,128)(2,1)S(1)}, u32[]{:S(2)}) copy-start(bf16[128,512]{1,0:T(8,128)(2,1)S(1)} %copy.150) | copy-start | bytes 393220
  143.8 4.6 %copy-start.67 = (bf16[896]{0:T(1024)(128)(2,1)}, bf16[896]{0:T(1024)(128)(2,1)S(1)}, u32[]{:S(2)}) copy-start(bf16[896]{0:T(1024)(128)(2,1)S(1)} %pad.72.clone) | copy-start | bytes 5380
  143.8 5.5 %copy-start.50 = (bf16[128,128]{1,0:T(8,128)(2,1)S(1)}, bf16[128,128]{1,0:T(8,128)(2,1)}, u32[]{:S(2)}) copy-start(bf16[128,128]{1,0:T(8,128)(2,1)} %get-tuple-element.140) | copy-start | bytes 98308
  145.8 3.6 %copy-start.51 = (bf16[128,128]{1,0:T(8,128)(2,1)S(1)}, bf16[128,128]{1,0:T(8,128)(2,1)}, u32[]{:S(2)}) copy-start(bf16[128,128]{1,0:T(8,128)(2,1)} %get-tuple-element.141) | copy-start | bytes 98308
  148.3 2.8 %copy-start.76 = (f32[256]{0:T(256)S(1)}, f32[256]{0:T(256)}, u32[]{:S(2)}) copy-start(f32[256]{0:T(256)} %get-tuple-element.92) | copy-start | bytes 3076
  148.4 2.8 %copy-start.77 = (f32[256]{0:T(256)S(1)}, f32[256]{0:T(256)}, u32[]{:S(2)}) copy-start(f32[256]{0:T(256)} %get-tuple-element.82) | copy-start | bytes 3076
  148.4 3.7 %copy-start.58 = (f32[640]{0:T(1024)S(1)}, f32[640]{0:T(1024)}, u32[]{:S(2)}) copy-start(f32[640]{0:T(1024)} %get-tuple-element.88) | copy-start | bytes 7684
  148.4 3.7 %copy-start.59 = (f32[640]{0:T(1024)S(1)}, f32[640]{0:T(1024)}, u32[]{:S(2)}) copy-start(f32[640]{0:T(1024)} %get-tuple-element.86) | copy-start | bytes 7684
  148.4 3.7 %copy-start.60 = (f32[640]{0:T(1024)S(1)}, f32[640]{0:T(1024)}, u32[]{:S(2)}) copy-start(f32[640]{0:T(1024)} %get-tuple-element.84) | copy-start | bytes 7684
  149.3 5.1 %copy-start.28 = (bf16[4,128,256]{1,2,0:T(8,128)(2,1)S(1)}, bf16[4,128,256]{1,2,0:T(8,128)(2,1)}, u32[]{:S(2)}) copy-start(bf16[4,128,256]{1,2,0:T(8,128)(2,1)} %copy.126) | copy-start | bytes 786436
  156.1 4.0 %copy-start.4 = (f32[128,640]{1,0:T(8,128)S(1)}, f32[128,640]{1,0:T(8,128)}, u32[]{:S(2)}) copy-start(f32[128,640]{1,0:T(8,128)} %copy-done.3) | copy-start | bytes 983044
  156.1 4.0 %copy-start.18 = (bf16[128,640]{1,0:T(8,128)(2,1)S(1)}, bf16[128,640]{1,0:T(8,128)(2,1)}, u32[]{:S(2)}) copy-start(bf16[128,640]{1,0:T(8,128)(2,1)} %param.23) | copy-start | bytes 491524
  156.1 4.0 %copy-start.20 = (bf16[128,1024]{1,0:T(8,128)(2,1)S(1)}, bf16[128,1024]{1,0:T(8,128)(2,1)}, u32[]{:S(2)}) copy-start(bf16[128,1024]{1,0:T(8,128)(2,1)} %copy-done.19) | copy-start | bytes 786436
  156.1 4.0 %copy-start.22 = (bf16[128,1024]{1,0:T(8,128)(2,1)S(1)}, bf16[128,1024]{1,0:T(8,128)(2,1)}, u32[]{:S(2)}) copy-start(bf16[128,1024]{1,0:T(8,128)(2,1)} %copy-done.21) | copy-start | bytes 786436
  156.1 4.0 %copy-start.66 = (f32[128]{0:T(128)S(1)}, f32[128]{0:T(128)}, u32[]{:S(2)}) copy-start(f32[128]{0:T(128)} %copy-done.65) | copy-start | bytes 1540
  156.1 4.0 %copy-start.69 = (f32[128]{0:T(128)S(1)}, f32[128]{0:T(128)}, u32[]{:S(2)}) copy-start(f32[128]{0:T(128)} %copy-done.68) | copy-start | bytes 1540
  156.1 4.0 %copy-start.79 = (f32[128]{0:T(128)S(1)}, f32[128]{0:T(128)}, u32[]{:S(2)}) copy-start(f32[128]{0:T(128)} %copy-done.78) | copy-start | bytes 1540
  (38 other events, 64.1 us)

commit v3 on v2

--- a/solution.py
+++ b/solution.py
@@ -351,11 +351,9 @@
     front, wide, tall, high = gather_parts(
         front, pair(gate, up), out.reshape(2, 32, 640), down.reshape(2, 64, 640)
     )
-    out = jnp.swapaxes(tall, 0, 1).reshape(1024, 640)
-    down = jnp.swapaxes(high, 0, 1).reshape(2048, 640)
     norms = front[0, :, :, 768:772].reshape(640, 4).T
     heads = front[0, :, :16, 772:774].reshape(256, 2).T
-    return (front.reshape(2, 640, 896), out, wide.reshape(2, 640, 2048), down, norms, heads)
+    return (front.reshape(2, 640, 896), tall, wide.reshape(2, 640, 2048), high, norms, heads)
 
 
 def gather_plain(weights, norm_gains, head_gains):
@@ -369,15 +367,13 @@
     return (pair(query, key, value, blank), out, pair(gate, up), down, norms, heads)
 
 
-def reduce_all(front, out, wide, down, norm_grad, head_grad):
+def reduce_all(front, tall, wide, high, norm_grad, head_grad):
     gains = jnp.pad(norm_grad.T, ((0, 0), (0, 124))) + jnp.pad(
         jnp.pad(head_grad.T.reshape(16, 16, 2), ((0, 0), (0, 24), (0, 0))).reshape(640, 2),
         ((0, 0), (4, 122)),
     )
     gains = gains.astype(jnp.bfloat16)
     front = lax.dynamic_update_slice(front, gains[None], (0, 0, 768))
-    tall = jnp.swapaxes(out.reshape(16, 2, 32, 640), 0, 1)
-    high = jnp.swapaxes(down.reshape(16, 2, 64, 640), 0, 1)
     summed = scatter_parts(
         front.reshape(2, 16, 40, 896), tall, wide.reshape(2, 16, 40, 2048), high
     )
@@ -539,11 +535,290 @@
     )
 
 
+def norm_forward(values, gain_row):
+    scale = lax.rsqrt(jnp.mean(values * values, axis=-1, keepdims=True) + EPSILON)
+    unit = values * scale
+    return unit, scale, unit * gain_row
+
+
+def norm_backward(unit, scale, gain_row, grad):
+    inner = grad * gain_row
+    back = scale * (inner - unit * jnp.mean(inner * unit, axis=-1, keepdims=True))
+    return back, jnp.sum(grad * unit, axis=0, keepdims=True)
+
+
+def head_forward(raw, gain_row, cos_part, sin_part):
+    unit, scale, scaled = norm_forward(raw, gain_row)
+    lead, second = scaled[:, :128], scaled[:, 128:]
+    turned = jnp.concatenate(
+        [lead * cos_part - second * sin_part, second * cos_part + lead * sin_part], axis=1
+    )
+    return unit, scale, turned
+
+
+def head_backward(unit, scale, gain_row, cos_part, sin_part, grad):
+    lead, second = grad[:, :128], grad[:, 128:]
+    back = jnp.concatenate(
+        [lead * cos_part + second * sin_part, second * cos_part - lead * sin_part], axis=1
+    )
+    return norm_backward(unit, scale, gain_row, back)
+
+
+def plain_dot(left, right):
+    return jnp.dot(left, right, preferred_element_type=jnp.float32)
+
+
+def layer_kernel(
+    tokens,
+    cotangent,
+    allowed,
+    live,
+    cosines,
+    sines,
+    norms,
+    heads,
+    front,
+    tall,
+    wide,
+    high,
+    mixed,
+    tokens_grad,
+    front_grad,
+    tall_grad,
+    wide_grad,
+    high_grad,
+    norms_grad,
+    heads_grad,
+    out_full,
+    down_full,
+    gate_pre,
+    up_pre,
+    acts,
+    total,
+):
+    low = jnp.bfloat16
+    shards = tall.shape[1]
+
+    @pl.loop(0, shards)
+    def _(j):
+        for h in (0, 1):
+            out_full[pl.ds(pl.multiple_of(j * 64 + h * 32, 32), 32), :] = tall[h, j]
+            down_full[pl.ds(pl.multiple_of(j * 128 + h * 64, 64), 64), :] = high[h, j]
+
+    gain = [norms[i : i + 1, :] for i in range(4)]
+    query_gain, key_gain = heads[0:1, :], heads[1:2, :]
+    cos_part, sin_part = cosines[...], sines[...]
+    x = tokens[...].astype(jnp.float32)
+    in_unit, in_scale, normed = norm_forward(x, gain[0])
+    input_low = normed.astype(low)
+    raw = [plain_dot(input_low, front[h]) for h in (0, 1)]
+    key_raw = jnp.concatenate([raw[0][:, 512:640], raw[1][:, 512:640]], axis=1)
+    value_low = jnp.concatenate([raw[0][:, 640:768], raw[1][:, 640:768]], axis=1).astype(low)
+    key_unit, key_scale, key_rot = head_forward(key_raw, key_gain, cos_part, sin_part)
+    key_low = key_rot.astype(low)
+    permit = allowed[...] > 0.5
+    kept = []
+    outputs = []
+    for n in range(HQ):
+        query_raw = raw[n // 2][:, n % 2 * HD : n % 2 * HD + HD]
+        unit, scale, turned = head_forward(query_raw, query_gain, cos_part, sin_part)
+        query_low = (turned * QUERY_SCALE).astype(low)
+        scores = jnp.where(permit, tail_dot(query_low, key_low), -1e30)
+        expo = jnp.exp(scores - jnp.max(scores, axis=-1, keepdims=True))
+        probs = expo / jnp.sum(expo, axis=-1, keepdims=True)
+        outputs.append(plain_dot(probs.astype(low), value_low).astype(low))
+        kept.append((unit, scale, query_low, probs))
+    attn_low = jnp.concatenate(outputs, axis=1)
+    post_unit, post_scale, post = norm_forward(plain_dot(attn_low, out_full[...]), gain[1])
+    resid = x + post
+    mid_unit, mid_scale, mid = norm_forward(resid, gain[2])
+    mid_low = mid.astype(low)
+
+    total[...] = jnp.zeros_like(total)
+    for h in (0, 1):
+
+        @pl.loop(0, 4)
+        def _(i):
+            here = pl.multiple_of(i * 256, 256)
+            there = pl.multiple_of(h * 1024 + i * 256, 256)
+            gate = plain_dot(mid_low, wide[h, :, pl.ds(here, 256)])
+            up = plain_dot(mid_low, wide[h, :, pl.ds(pl.multiple_of(1024 + here, 256), 256)])
+            bend = jnp.tanh(0.7978845608028654 * (gate + 0.044715 * gate * gate * gate))
+            act = (0.5 * gate * (1.0 + bend) * up).astype(low)
+            gate_pre[:, pl.ds(there, 256)] = gate
+            up_pre[:, pl.ds(there, 256)] = up
+            acts[:, pl.ds(there, 256)] = act
+            total[...] += plain_dot(act, down_full[pl.ds(there, 256), :])
+
+    last_unit, last_scale, last = norm_forward(total[...], gain[3])
+    alive = live[...]
+    mixed[...] = ((resid + last) * alive).astype(low)
+    out_grad = cotangent[...].astype(jnp.float32) * alive
+    down_grad, last_gain = norm_backward(last_unit, last_scale, gain[3], out_grad)
+    down_low = down_grad.astype(low)
+
+    total[...] = jnp.zeros_like(total)
+    for h in (0, 1):
+
+        @pl.loop(0, 4)
+        def _(i):
+            here = pl.multiple_of(i * 256, 256)
+            beside = pl.multiple_of(1024 + here, 256)
+            there = pl.multiple_of(h * 1024 + i * 256, 256)
+            gate = gate_pre[:, pl.ds(there, 256)]
+            up = up_pre[:, pl.ds(there, 256)]
+            act_grad = tail_dot(down_low, down_full[pl.ds(there, 256), :])
+            term = lead_dot(acts[:, pl.ds(there, 256)], down_low).astype(low)
+            for k in (0, 1):
+                for part in (0, 1):
+                    start = k * 128 + part * 64
+                    high_grad[part, h * 8 + i * 2 + k] = term[start : start + 64]
+            square = gate * gate
+            bend = jnp.tanh(0.7978845608028654 * gate * (1.0 + 0.044715 * square))
+            slope = 0.5 * (1.0 + bend) + 0.5 * gate * (1.0 - bend * bend) * (
+                0.7978845608028654 * (1.0 + 0.134145 * square)
+            )
+            gate_low = (act_grad * up * slope).astype(low)
+            up_low = (act_grad * (0.5 * gate * (1.0 + bend))).astype(low)
+            wide_grad[h, :, pl.ds(here, 256)] = lead_dot(mid_low, gate_low).astype(low)
+            wide_grad[h, :, pl.ds(beside, 256)] = lead_dot(mid_low, up_low).astype(low)
+            total[...] += tail_dot(gate_low, wide[h, :, pl.ds(here, 256)]) + tail_dot(
+                up_low, wide[h, :, pl.ds(beside, 256)]
+            )
+
+    mid_back, mid_gain = norm_backward(mid_unit, mid_scale, gain[2], total[...])
+    resid_grad = out_grad + mid_back
+    attn_grad, post_gain = norm_backward(post_unit, post_scale, gain[1], resid_grad)
+    attn_grad_low = attn_grad.astype(low)
+    term = lead_dot(attn_low, attn_grad_low).astype(low)
+    for j in range(shards):
+        for part in (0, 1):
+            tall_grad[part, j] = term[j * 64 + part * 32 : j * 64 + part * 32 + 32]
+
+    value_grad = jnp.zeros((x.shape[0], HD), jnp.float32)
+    key_grad = jnp.zeros((x.shape[0], HD), jnp.float32)
+    query_gain_grad = jnp.zeros((1, HD), jnp.float32)
+    query_grads = []
+    for n in range(HQ):
+        unit, scale, query_low, probs = kept[n]
+        back = tail_dot(attn_grad_low, out_full[n * HD : (n + 1) * HD, :]).astype(low)
+        value_grad += lead_dot(probs.astype(low), back)
+        prob_grad = tail_dot(back, value_low)
+        score_grad = (
+            probs * (prob_grad - jnp.sum(probs * prob_grad, axis=-1, keepdims=True))
+        ).astype(low)
+        key_grad += lead_dot(score_grad, query_low)
+        query_grad, gain_term = head_backward(
+            unit,
+            scale,
+            query_gain,
+            cos_part,
+            sin_part,
+            plain_dot(score_grad, key_low) * QUERY_SCALE,
+        )
+        query_gain_grad += gain_term
+        query_grads.append(query_grad.astype(low))
+    key_raw_grad, key_gain_grad = head_backward(
+        key_unit, key_scale, key_gain, cos_part, sin_part, key_grad
+    )
+    key_raw_low, value_grad_low = key_raw_grad.astype(low), value_grad.astype(low)
+    in_grad = jnp.zeros(x.shape, jnp.float32)
+    for h in (0, 1):
+        raw_grad = jnp.concatenate(
+            query_grads[2 * h : 2 * h + 2]
+            + [
+                key_raw_low[:, h * 128 : h * 128 + 128],
+                value_grad_low[:, h * 128 : h * 128 + 128],
+            ],
+            axis=1,
+        )
+        in_grad += tail_dot(raw_grad, front[h, :, 0:768])
+        front_grad[h, :, 0:768] = lead_dot(input_low, raw_grad).astype(low)
+        front_grad[h, :, 768:896] = jnp.zeros((x.shape[1], 128), low)
+    in_back, in_gain = norm_backward(in_unit, in_scale, gain[0], in_grad)
+    tokens_grad[...] = (resid_grad + in_back).astype(low)
+    for n, row in enumerate((in_gain, post_gain, mid_gain, last_gain)):
+        norms_grad[n : n + 1, :] = row
+    heads_grad[0:1, :] = query_gain_grad
+    heads_grad[1:2, :] = key_gain_grad
+
+
+def local_fused(
+    tokens,
+    lengths,
+    w_query,
+    w_key,
+    w_value,
+    w_out,
+    w_gate,
+    w_up,
+    w_down,
+    norm_gains,
+    head_gains,
+    cotangent,
+):
+    rows, width = tokens.shape
+    row_index = jnp.arange(rows, dtype=jnp.int32)
+    segment, position = layout(lengths[0], row_index)
+    live = (segment < 2).astype(jnp.float32)[:, None]
+    cos_part, sin_part = angles(position, HD)
+    allowed = causal_mask(segment, row_index).astype(jnp.float32)
+    front, tall, wide, high, norms, heads = gather_all(
+        (w_query, w_key, w_value, w_out, w_gate, w_up, w_down), norm_gains, head_gains
+    )
+    low = jnp.bfloat16
+    vmem = pl.BlockSpec(memory_space=pltpu.VMEM)
+    shapes = (
+        (tokens.shape, low),
+        (tokens.shape, low),
+        (front.shape, low),
+        (tall.shape, low),
+        (wide.shape, low),
+        (high.shape, low),
+        (norms.shape, jnp.float32),
+        (heads.shape, jnp.float32),
+    )
+    hidden = wide.shape[2]
+    results = pl.pallas_call(
+        layer_kernel,
+        out_shape=tuple(jax.ShapeDtypeStruct(*s) for s in shapes),
+        in_specs=[vmem] * 12,
+        out_specs=(vmem,) * 8,
+        scratch_shapes=[
+            pltpu.VMEM((HQ * HD, width), low),
+            pltpu.VMEM((hidden, width), low),
+            pltpu.VMEM((rows, hidden), jnp.float32),
+            pltpu.VMEM((rows, hidden), jnp.float32),
+            pltpu.VMEM((rows, hidden), low),
+            pltpu.VMEM((rows, width), jnp.float32),
+        ],
+        compiler_params=pltpu.CompilerParams(vmem_limit_bytes=52 * 1024 * 1024),
+        name="layer",
+    )(
+        tokens,
+        cotangent,
+        allowed,
+        live,
+        cos_part,
+        sin_part,
+        norms.astype(jnp.float32),
+        heads.astype(jnp.float32),
+        front,
+        tall,
+        wide,
+        high,
+    )
+    mixed, tokens_grad, grad_front, grad_tall, grad_wide, grad_high, norm_grad, head_grad = results
+    return (mixed, tokens_grad) + reduce_all(
+        grad_front, grad_tall, grad_wide, grad_high, norm_grad, head_grad
+    )
+
+
 def solution(mesh):
     if mesh.shape["rep"] == 2 and mesh.shape["shard"] == 16:
-        steps = (gather_all, reduce_all)
+        step = local_fused
     else:
-        steps = (gather_plain, reduce_plain)
+        step = partial(local, gather_plain, reduce_plain)
     placed = (
         P(("rep", "shard"), None),
         P(("rep", "shard"), None),
@@ -559,7 +834,7 @@
         P(("rep", "shard"), None),
     )
     return jax.shard_map(
-        partial(local, *steps),
+        step,
         mesh=mesh,
         in_specs=placed,
         out_specs=(

time: 251 us -> 205 us (0.82)
  local copies, waits for them, and re-layouts: 41 us -> 10.9 us
  Pallas kernels: 158 us -> 181 us
  matrix products: 21.1 us -> 0 us
  other arithmetic: 24.3 us -> 8.99 us
    pallas_call x0 -> x1, Pallas kernels: none -> 22.4 us  [local_fused(): pl.pallas_call(layer_kernel, out_shape=tuple((jax.ShapeDtypeStruct(*s) fo...]
    dot_general x21 -> x0, matrix products: 18.8 us -> none  [the longest x7 7.78 us: tail_dot(): lax.dot_general(left, right, (((1,), (1,)), ((), ())), preferred_element_...]
    slice x10 -> x0, local copies, waits for them, and re-layouts: 7.38 us -> none  [the longest x1 2.03 us: local(): wide[h]]
    unnamed x177 -> x7, local copies, waits for them, and re-layouts: 9.23 us -> 2.18 us
    reduce_sum x8 -> x0, other arithmetic: 5.51 us -> none  [the longest x4 3.83 us: rms_norm(): values * lax.rsqrt(jnp.mean(values * values, axis=-1, keepdims=True) + EP...]
    transpose x2 -> x0, local copies, waits for them, and re-layouts: 5.26 us -> none  [the longest x1 3.7 us: gather_all(): down = jnp.swapaxes(high, 0, 1).reshape(2048, 640)]
    reshape x10 -> x1, local copies, waits for them, and re-layouts: 4.92 us -> 0.09 us  [reduce_all(): jnp.pad(head_grad.T.reshape(16, 16, 2), ((0, 0), (0, 24), (0, 0)))]
    slice x7 -> x4, local copies, waits for them, and re-layouts: 6.4 us -> 3.41 us  [pair(): c[:, h * c.shape[1] // 2:(h + 1) * c.shape[1] // 2]]
where the time goes in v3:
time: 205 us; the launch traced here: 203 us
  Pallas kernels  181 us (88%)
  local copies, waits for them, and re-layouts  10.9 us (5%)
  other arithmetic  8.99 us (4%)
  between operations  2.08 us (1%)
    pallas_call x1, Pallas kernels, gather_parts(): pl.pallas_call(gather_kernel, out_shape=tuple((jax.ShapeDtypeStruct((2, 1...  79.4 us
    pallas_call x1, Pallas kernels, scatter_parts(): pl.pallas_call(scatter_kernel, out_shape=tuple((jax.ShapeDtypeStruct((2,)...  78.8 us
    pallas_call x1, Pallas kernels, local_fused(): pl.pallas_call(layer_kernel, out_shape=tuple((jax.ShapeDtypeStruct(*s) fo...  22.4 us

profile of v3, /device:TPU:9, one launch (start us, length us, event | category | flops | bytes accessed | tf_op | source)
XLA Modules:
  0.0 202.5 jit_solution(6302409956825062393)
XLA Ops:
  0.7 1.3 fusion.14
  3.3 0.7 fusion.6
  3.9 0.7 copy.32
  4.7 0.8 copy.31
  5.5 0.8 fusion.12
  6.3 0.7 fusion.13
  7.0 0.7 fusion.5.live
  7.6 0.1 fusion.4.allowed
  7.7 0.8 fusion.11
  8.6 0.7 pad_maximum_fusion.4.refs_0_
  9.2 0.0 copy-start
  9.2 0.0 copy-start.1
  9.2 0.3 multiply_sine_fusion
  9.6 0.9 fusion.9
  10.5 0.9 fusion.10
  11.5 0.8 pad_maximum_fusion.refs_1_
  12.2 79.4 %gather_weights.1 = (bf16[2,16,40,896]{3,2,1,0:T(8,128)(2,1)}, bf16[2,16,40,2048]{3,2,1,0:T(8,128)(2,1)}, bf16[2,16,32,640]{3,2,1,0:T(8,128)(2,1)}, bf16[2,16,64,640]{3,2,1,0:T(8,128)(2,1)}) custom-call(bf16[2,40,896]{2,1,0:T(8,128)(2,1)} %pad_maximum_fusion.4.refs_0_, bf16[2,40,2048]{2,1,0:T(8,128)(2,1)} %pad_maximum_fusion.refs_1_, ...), custom_call_target="tpu_custom_call" | custom-call | tf_op jit(solution)/shard_map/gather_weights/pallas_call | solution.py:204
  91.7 0.9 slice.93
  92.6 0.1 copy.39
  92.7 0.9 slice.92
  93.7 0.1 copy.38
  93.8 0.0 copy-done
  93.8 0.0 copy-done.1
  93.8 22.4 %layer.1 = (bf16[128,640]{1,0:T(8,128)(2,1)}, bf16[128,640]{1,0:T(8,128)(2,1)}, bf16[2,640,896]{2,1,0:T(8,128)(2,1)}, bf16[2,16,32,640]{3,2,1,0:T(8,128)(2,1)S(1...) custom-call(bf16[128,640]{1,0:T(8,128)(2,1)S(1)} %copy-done, ...), custom_call_target="tpu_custom_call" | custom-call | tf_op jit(solution)/shard_map/layer/pallas_call | solution.py:782
  116.2 0.1 reshape.127
  116.3 0.1 reshape.128
  116.4 0.2 copy.35
  116.6 0.7 constant_dynamic-update-slice_fusion
  117.3 78.8 %scatter_grads.1 = (bf16[2,40,896]{2,1,0:T(8,128)(2,1)S(1)}, bf16[2,32,640]{2,1,0:T(8,128)(2,1)S(1)}, bf16[2,40,2048]{2,1,0:T(8,128)(2,1)S(1)}, bf16[2,64,640]{2,1,0:T(8,128)(2,1)S(1)}) custom-call(bf16[2,16,40,896]{3,2,1,0:T(8,128)(2,1)} %bitcast.74, bf16[2,16,32,640]{3,2,1,0:T(8,128)(2,1)S(1)} %get-tuple-element.36.refs_1_, ...), custom_call_target="tpu_custom_call" | custom-call | tf_op jit(solution)/shard_map/scatter_grads/pallas_call | solution.py:314
  196.1 0.1 slice.117
  196.2 0.6 copy.36
  196.8 0.7 bitcast_convert_fusion.2
  197.5 0.7 copy.37
  198.2 0.7 pad_maximum_fusion.3
  198.9 0.6 pad_maximum_fusion.8
  199.5 0.6 pad_maximum_fusion.7
  200.1 0.8 bitcast_convert_fusion
  201.0 0.1 slice_bitcast_fusion.1
  201.0 0.7 pad_maximum_fusion.2
  201.8 0.7 pad_maximum_fusion.1
  (12 shorter events, 0.2 us)
Async XLA Ops:
  9.2 84.6 %copy-start = (bf16[128,640]{1,0:T(8,128)(2,1)S(1)}, bf16[128,640]{1,0:T(8,128)(2,1)}, u32[]{:S(2)}) copy-start(bf16[128,640]{1,0:T(8,128)(2,1)} %tokens.1) | copy-start | bytes 491524
  9.2 84.6 %copy-start.1 = (bf16[128,640]{1,0:T(8,128)(2,1)S(1)}, bf16[128,640]{1,0:T(8,128)(2,1)}, u32[]{:S(2)}) copy-start(bf16[128,640]{1,0:T(8,128)(2,1)} %cotangent.1) | copy-start | bytes 491524
